TPU v7x, 128 devices: a whole 4x4x4 slice. The times are simulated.
128 devices in a mesh: stream: 4 (over y), tile: 32 (over x, z, core).
Axes of the slice: x: 4, y: 4, z: 4, core: 2. Of those that a mesh axis runs over, the one named last changes fastest.
Arguments:
- concentration: bfloat16 [2, 768, 1024, 128], P(None, 'stream', 'tile'), may hold values from 0.29882812 to 3
- potential: bfloat16 [768, 1024, 128], P('stream', 'tile'), may hold values from -4 to 4
- diffusivity: bfloat16 [768, 1024, 128], P('stream', 'tile'), may hold values from 0.5 to 2
- spacer: int32 [768, 1024, 128], P('stream', 'tile'), may hold values 0 or 1
- velocity: bfloat16 [3, 768, 1024, 128], P(None, 'stream', 'tile'), may hold values from -4 to 4
- balance_plan: int32 [3072, 1], P(('stream', 'tile')), may hold values from 0 to 31; in each aligned block of 24 rows (0 to 23, 24 to 47, ...) at most 2 rows name the same one
Outputs:
- concentration_next: bfloat16 [2, 768, 1024, 128], P(None, 'stream', 'tile')
- velocity_next: bfloat16 [3, 768, 1024, 128], P(None, 'stream', 'tile')
- owned_charge: bfloat16 [8192, 32, 1024], P(('stream', 'tile'))
Inputs may be any that keep to these rules, and one draw needn't show every extreme that they name: 1 marks fluid, 0 a spacer filament. `balance_plan`: the 24 blocks of one slab tile (aligned rows of one device) name owners among the 32 tiles of the same slab; at most 2 of them name the same owner, and some slab tile has exactly 2 with one owner.
All inputs are finite; a program needn't handle non-finite values. No bound on the sum of `spacer` on one device may be relied on, other than what follows from the above.
Results may differ from a plain program's by a relative error of at most 0.011.
Values may be sent and summed in bfloat16 or wider, within the bound.
A program may use at most 256 MiB of HBM per device.

v0:
```python
import jax
import jax.numpy as jnp
from jax import lax
from jax.sharding import PartitionSpec as P

BLK = 32
BX = 6
BZ = 4


ion_step = 0.04
flow_step = 0.1
viscosity = 0.5
species_diff = (1.0, 1.5)
species_charge = (1.0, -1.0)


def with_halo(block, sides, width):
    for axis, dim in sides:
        count = lax.axis_size(axis)
        forward = [(i, i + 1) for i in range(count - 1)]
        forward.append((count - 1, 0))
        backward = [(target, source) for source, target in forward]
        low = lax.ppermute(
            lax.slice_in_dim(block, block.shape[dim] - width, None, axis=dim), axis, forward
        )
        high = lax.ppermute(lax.slice_in_dim(block, 0, width, axis=dim), axis, backward)
        block = jnp.concatenate([low, block, high], axis=dim)
    return block


def neighbor_view(source, axis_number, offset):
    first = [1, 1, 1]
    first[axis_number] = 1 + offset
    return source[
        first[0] : first[0] + source.shape[0] - 2,
        first[1] : first[1] + source.shape[1] - 2,
        first[2] : first[2] + source.shape[2] - 2,
    ]


def interior_view(source):
    return source[1:-1, 1:-1, 1:-1]


def ion_update(padded):
    fields = padded.astype(jnp.float32)
    electric = fields[2]
    openness = fields[3]
    open_mid = interior_view(openness)
    pot_mid = interior_view(electric)
    updated = []
    for species in range(2):
        density = fields[species]
        dens_mid = interior_view(density)
        running = jnp.zeros_like(dens_mid)
        for axis_number in range(3):
            for offset in (-1, 1):
                dens_near = neighbor_view(density, axis_number, offset)
                pot_near = neighbor_view(electric, axis_number, offset)
                face_coef = jnp.sqrt(open_mid * neighbor_view(openness, axis_number, offset))
                running = running + face_coef * (
                    dens_near
                    - dens_mid
                    + species_charge[species] * 0.5 * (dens_mid + dens_near) * (pot_near - pot_mid)
                )
        updated.append(dens_mid + ion_step * species_diff[species] * running)
    return jnp.stack(updated)


def flow_update(flow_pad, pot_pad, charge, fluid_cells):
    flow_field = flow_pad.astype(jnp.float32)
    electric = pot_pad.astype(jnp.float32)
    middle = [interior_view(flow_field[component]) for component in range(3)]
    result = []
    for component in range(3):
        advect = jnp.zeros_like(middle[component])
        diffuse = -6.0 * middle[component]
        for axis_number in range(3):
            forward = neighbor_view(flow_field[component], axis_number, 1)
            backward = neighbor_view(flow_field[component], axis_number, -1)
            advect = advect + middle[axis_number] * 0.5 * (forward - backward)
            diffuse = diffuse + forward + backward
        field_part = -0.5 * (
            neighbor_view(electric, component, 1) - neighbor_view(electric, component, -1)
        )
        result.append(
            fluid_cells
            * (middle[component] + flow_step * (viscosity * diffuse - advect + charge * field_part))
        )
    return jnp.stack(result).astype(jnp.bfloat16)


def height_pad(source):
    return jnp.pad(source, ((0, 0), (0, 0), (0, 0), (1, 1)))


def per_device(concentration, potential, diffusivity, spacer, velocity, balance_plan):
    tiles = lax.axis_size("tile")
    count = balance_plan.shape[0]
    capacity = max(2, (2 * count + tiles - 1) // tiles)
    slots = tiles * capacity
    openness = jnp.where(spacer > 0, diffusivity, jnp.zeros_like(diffusivity))
    moving = jnp.where(spacer[None] > 0, velocity, jnp.zeros_like(velocity))
    fluid_cells = (spacer > 0).astype(jnp.float32)
    ions = jnp.concatenate([concentration, potential[None], openness[None]], axis=0)
    ion_pad = height_pad(with_halo(ions, (("stream", 1), ("tile", 2)), 1))
    owners = balance_plan[:, 0]
    same_owner = owners[:, None] == owners[None, :]
    earlier = (
        jnp.arange(count, dtype=jnp.int32)[:, None] < jnp.arange(count, dtype=jnp.int32)[None, :]
    )
    ranking = jnp.sum(jnp.logical_and(same_owner, earlier).astype(jnp.int32), axis=0)
    target = owners * capacity + ranking
    conc_next = ion_update(ion_pad).astype(jnp.bfloat16)
    charge = conc_next[0].astype(jnp.float32) - conc_next[1].astype(jnp.float32)
    charge_blocks = (
        charge.astype(jnp.bfloat16)
        .reshape(BX, BLK, BLK, BZ, BLK)
        .transpose(0, 3, 1, 2, 4)
        .reshape(count, BLK, BLK * BLK)
    )
    outgoing = (
        jnp.zeros((slots, BLK, BLK * BLK), jnp.bfloat16)
        .at[target]
        .set(charge_blocks)
        .reshape(tiles, capacity, BLK, BLK * BLK)
    )
    owned_out = lax.all_to_all(outgoing, "tile", split_axis=0, concat_axis=0, tiled=True).reshape(
        slots, BLK, BLK * BLK
    )
    flow_pad = height_pad(with_halo(moving, (("stream", 1), ("tile", 2)), 1))
    flow_next = flow_update(flow_pad, ion_pad[2], charge, fluid_cells)
    return (conc_next, flow_next, owned_out)


def solution(mesh):
    placed = (
        P(None, "stream", "tile", None),
        P("stream", "tile", None),
        P("stream", "tile", None),
        P("stream", "tile", None),
        P(None, "stream", "tile", None),
        P(("stream", "tile"), None),
    )
    return jax.shard_map(
        per_device,
        mesh=mesh,
        in_specs=placed,
        out_specs=(
            P(None, "stream", "tile", None),
            P(None, "stream", "tile", None),
            P(("stream", "tile"), None, None),
        ),
        check_vma=False,
    )
```

profile of v0, /device:TPU:1, one launch (start us, length us, event | category | flops | bytes accessed | tf_op | source)
XLA Modules:
  0.0 359.1 jit_solution(16104512424445584892)
XLA Ops:
  0.7 3.2 select_bitcast_fusion
  3.9 0.5 copy-done
  4.4 2.2 collective-permute-start
  6.6 1.5 collective-permute-start.1
  8.2 1.0 broadcast_select_fusion
  9.1 0.8 collective-permute-start.4
  9.9 1.9 collective-permute-start.5
  12.0 1.1 collective-permute-done.4
  13.1 0.5 pad_maximum_fusion.9
  13.6 3.8 %collective-permute-start.6 = (bf16[3,194,1,128]{3,2,1,0:T(2,128)(2,1)S(1)}, bf16[3,194,1,128]{3,2,1,0:T(2,128)(2,1)S(1)}, u32[]{:S(2)}, u32[]{:S(2)}) collective-permute-start(bf16[3,194,1,128]{3,2,1,0:T(2,128)(2,1)S(1)} %get-tuple-element.21), channel_id=1, source_target_pairs={{0,1},{1,2},{2,3},{3,4},{4,5},{5,6},{6,7},{7,8},{8,9},{9,10},{10,1... | collective-permute-start | bytes 446984 | tf_op jit(solution)/shard_map/ppermute | solution.py:24
  17.4 1.5 pad_maximum_fusion.6
  19.0 1.8 collective-permute-start.2
  20.7 2.0 collective-permute-start.3
  22.7 1.2 collective-permute-done.7
  23.9 19.1 %fusion.11 = f32[3,194,34,130]{3,2,1,0:T(8,128)} fusion(bf16[3,194,1,128]{3,2,1,0:T(2,128)(2,1)S(1)} %collective-permute-done.7, bf16[3,194,1,128]{3,2,1,0:T(2,128)(2,1)S(1)} %collective-permute-done.6, bf16[3,1,32,128]{3,2,1,0:T(8,128)(2,1)S(1)} %collective-permute-done.5, bf16[3,192,32,128]{3,2,1,0:T(8,128)(2,1)S(1)} %broadcast_select_fusion, ...), kind=kLoop, calls=%fused_computation.19 | loop fusion | flops 46303920 | bytes 15355488 | tf_op jit(solution)/shard_map/convert_element_type | solution.py:72
  43.0 16.7 %slice_bitcast_fusion = (f32[194,34,130]{2,1,0:T(8,128)}, f32[194,34,130]{2,1,0:T(8,128)}, f32[194,34,130]{2,1,0:T(8,128)}) fusion(f32[3,194,34,130]{3,2,1,0:T(8,128)} %fusion.11), kind=kLoop, calls=%fused_computation.26 | loop fusion | bytes 20579520 | tf_op jit(solution)/shard_map/squeeze | solution.py:74
  59.7 32.1 %fusion.55 = (f32[4,194,34,130]{3,2,1,0:T(8,128)}, bf16[4,194,34,130]{3,2,1,0:T(8,128)(2,1)}) fusion(bf16[4,194,1,128]{3,2,1,0:T(2,128)(2,1)S(1)} %collective-permute-done.3, bf16[4,1,32,128]{3,2,1,0:T(8,128)(2,1)S(1)} %collective-permute-done.1, bf16[1,192,32,128]{3,2,1,0:T(8,128)(2,1)S(1)} %get-tuple-element.8, bf16[1,192,32,128]{3,2,1,0:T(8,128)(2,1)S(1)} %bitcast.64, ...), kind=kLoop, calls=%fused_computation.112 | loop fusion | flops 85748000 | bytes 27333824 | tf_op jit(solution)/shard_map/convert_element_type | solution.py:47
  91.8 22.4 %slice_bitcast_fusion.3 = (f32[194,34,130]{2,1,0:T(8,128)}, f32[194,34,130]{2,1,0:T(8,128)}, f32[194,34,130]{2,1,0:T(8,128)}, f32[194,34,130]{2,1,0:T(8,128)}) fusion(f32[4,194,34,130]{3,2,1,0:T(8,128)} %get-tuple-element.6), kind=kLoop, calls=%fused_computation.29 | loop fusion | bytes 27439360 | tf_op jit(solution)/shard_map/squeeze | solution.py:54
  114.1 5.8 %fusion.17 = f32[194,34,130]{2,1,0:T(8,128)} fusion(bf16[4,194,34,130]{3,2,1,0:T(8,128)(2,1)} %get-tuple-element.7), kind=kLoop, calls=%fused_computation.37 | loop fusion | flops 857480 | bytes 5144880 | tf_op jit(solution)/shard_map/convert_element_type | solution.py:73
  119.9 86.4 %fusion.45 = (bf16[1,192,32,128]{3,2,1,0:T(8,128)(2,1)}, bf16[1,192,32,128]{3,2,1,0:T(8,128)(2,1)S(1)}, bf16[1,192,32,128]{3,2,1,0:T(8,128)(2,1)S(1)}) fusion(f32[194,34,130]{2,1,0:T(8,128)} %get-tuple-element.11, f32[194,34,130]{2,1,0:T(8,128)} %get-tuple-element.13, f32[194,34,130]{2,1,0:T(8,128)} %get-tuple-element.12, f32[194,34,130]{2,1,0:T(8,128)} %get-tuple-element.10), kind=kLoop, calls=%fused_computation.87 | loop fusion | flops 81788928 | bytes 92798976 | tf_op jit(solution)/shard_map/convert_element_type | solution.py:118
  206.3 9.0 %convert_element_type.49 = bf16[6,32,32,4,32]{4,3,2,1,0:T(4,128)(2,1)} reshape(bf16[1,192,32,128]{3,2,1,0:T(8,128)(2,1)} %get-tuple-element.3) | data formatting | bytes 3145728 | tf_op jit(solution)/shard_map/convert_element_type | solution.py:118
  215.3 6.7 %copy.12 = bf16[6,32,32,4,32]{4,2,1,3,0:T(8,128)(2,1)} copy(bf16[6,32,32,4,32]{4,3,2,1,0:T(4,128)(2,1)} %convert_element_type.49) | data formatting | bytes 3145728 | tf_op jit(solution)/shard_map/convert_element_type | solution.py:118
  222.0 9.7 %reshape.39 = bf16[24,32,1024]{2,1,0:T(8,128)(2,1)} reshape(bf16[6,4,32,32,32]{4,3,2,1,0:T(8,128)(2,1)} %bitcast.60) | data formatting | bytes 3145728 | tf_op jit(solution)/shard_map/reshape | solution.py:121
  231.7 2.5 broadcast_in_dim.32
  234.2 6.0 %scatter_fusion = bf16[64,32,1024]{2,1,0:T(8,128)(2,1)} fusion(bf16[64,32,1024]{2,1,0:T(8,128)(2,1)} %broadcast_in_dim.32, s32[24]{0:T(128)S(1)} %fusion.52, bf16[24,32,1024]{2,1,0:T(8,128)(2,1)} %reshape.39), kind=kCustom, calls=%fused_computation | custom fusion | bytes 4718688 | tf_op jit(solution)/shard_map/scatter | solution.py:126
  240.2 8.3 %all-to-all-start = ((bf16[32,2,32,1024]{3,2,1,0:T(8,128)(2,1)}), bf16[32,2,32,1024]{3,2,1,0:T(8,128)(2,1)}, u32[]{:S(2)}, u32[]{:S(2)}) async-start(bf16[32,2,32,1024]{3,2,1,0:T(8,128)(2,1)} %bitcast.61), calls=%async_computation | async-start | bytes 8388608 | tf_op jit(solution)/shard_map/all_to_all | solution.py:129
  248.5 33.4 %fusion.46 = bf16[1,192,32,128]{3,2,1,0:T(8,128)(2,1)} fusion(pred[192,32,128]{2,1,0:T(8,128)(4,1)} %copy-done.1, f32[194,34,130]{2,1,0:T(8,128)} %fusion.17, bf16[1,192,32,128]{3,2,1,0:T(8,128)(2,1)S(1)} %get-tuple-element.5, bf16[1,192,32,128]{3,2,1,0:T(8,128)(2,1)S(1)} %get-tuple-element.4, f32[194,34,130]{2,1,0:T(8,128)} %get-tuple-element.14, ...), kind=kLoop, calls=%fused_computation.90 | loop fusion | flops 24379392 | bytes 40108032 | tf_op jit(solution)/shard_map/stack | solution.py:91
  281.9 1.9 pad_maximum_fusion.1
  283.8 32.3 %fusion.47 = bf16[1,192,32,128]{3,2,1,0:T(8,128)(2,1)} fusion(pred[192,32,128]{2,1,0:T(8,128)(4,1)} %copy-done.1, f32[194,34,130]{2,1,0:T(8,128)} %fusion.17, bf16[1,192,32,128]{3,2,1,0:T(8,128)(2,1)S(1)} %get-tuple-element.5, bf16[1,192,32,128]{3,2,1,0:T(8,128)(2,1)S(1)} %get-tuple-element.4, f32[194,34,130]{2,1,0:T(8,128)} %get-tuple-element.14, ...), kind=kLoop, calls=%fused_computation.91 | loop fusion | flops 24379392 | bytes 40108032 | tf_op jit(solution)/shard_map/stack | solution.py:91
  316.1 32.9 %fusion.48 = bf16[1,192,32,128]{3,2,1,0:T(8,128)(2,1)} fusion(pred[192,32,128]{2,1,0:T(8,128)(4,1)} %copy-done.1, f32[194,34,130]{2,1,0:T(8,128)} %fusion.17, bf16[1,192,32,128]{3,2,1,0:T(8,128)(2,1)S(1)} %get-tuple-element.5, bf16[1,192,32,128]{3,2,1,0:T(8,128)(2,1)S(1)} %get-tuple-element.4, f32[194,34,130]{2,1,0:T(8,128)} %get-tuple-element.15, ...), kind=kLoop, calls=%fused_computation.92 | loop fusion | flops 24379392 | bytes 40108032 | tf_op jit(solution)/shard_map/stack | solution.py:91
  349.0 5.0 %pad_maximum_fusion = bf16[3,192,32,128]{3,2,1,0:T(8,128)(2,1)} fusion(bf16[1,192,32,128]{3,2,1,0:T(8,128)(2,1)} %fusion.48, bf16[1,192,32,128]{3,2,1,0:T(8,128)(2,1)} %fusion.47, bf16[1,192,32,128]{3,2,1,0:T(8,128)(2,1)} %fusion.46), kind=kLoop, calls=%fused_computation.34 | loop fusion | flops 4718592 | bytes 9437184 | tf_op jit(solution)/shard_map/stack | solution.py:91
  354.1 5.0 %copy.15 = bf16[64,32,1024]{2,1,0:T(8,128)(2,1)} copy(bf16[64,32,1024]{2,1,0:T(8,128)(2,1)} %bitcast.22) | data formatting | bytes 8388608
  (21 shorter events, 0.2 us)
Async XLA Ops:
  0.6 3.2 copy-start.2
  0.6 3.8 %copy-start = (bf16[2,192,32,128]{3,2,1,0:T(8,128)(2,1)S(1)}, bf16[2,192,32,128]{3,2,1,0:T(8,128)(2,1)}, u32[]{:S(2)}) copy-start(bf16[2,192,32,128]{3,2,1,0:T(8,128)(2,1)} %param.6) | copy-start | bytes 9437188
  3.9 4.3 %copy-start.1 = (pred[192,32,128]{2,1,0:T(8,128)(4,1)}, pred[192,32,128]{2,1,0:T(8,128)(4,1)S(1)}, u32[]{:S(2)}) copy-start(pred[192,32,128]{2,1,0:T(8,128)(4,1)S(1)} %get-tuple-element.9) | copy-start | bytes 2359300
  4.4 3.7 %copy-start.3 = (bf16[3,192,32,128]{3,2,1,0:T(8,128)(2,1)S(1)}, bf16[3,192,32,128]{3,2,1,0:T(8,128)(2,1)}, u32[]{:S(2)}) copy-start(bf16[3,192,32,128]{3,2,1,0:T(8,128)(2,1)} %param.10) | copy-start | bytes 14155780
  4.4 13.0 %collective-permute-start = (bf16[4,1,32,128]{3,2,1,0:T(8,128)(2,1)S(1)}, bf16[4,1,32,128]{3,2,1,0:T(8,128)(2,1)S(1)}, u32[]{:S(2)}, u32[]{:S(2)}) collective-permute-start(bf16[4,1,32,128]{3,2,1,0:T(8,128)(2,1)S(1)} %get-tuple-element.19), channel_id=1, source_target_pairs={{0,32},{32,64},{64,96},{96,0},{1,33},{33,65},{65,97},{97,1},{2,34}... | collective-permute-start | bytes 98312 | tf_op jit(solution)/shard_map/ppermute | solution.py:24
  6.6 10.8 %collective-permute-start.1 = (bf16[4,1,32,128]{3,2,1,0:T(8,128)(2,1)S(1)}, bf16[4,1,32,128]{3,2,1,0:T(8,128)(2,1)S(1)}, u32[]{:S(2)}, u32[]{:S(2)}) collective-permute-start(bf16[4,1,32,128]{3,2,1,0:T(8,128)(2,1)S(1)} %get-tuple-element.20), channel_id=1, source_target_pairs={{32,0},{64,32},{96,64},{0,96},{33,1},{65,33},{97,65},{1,97},{34,2}... | collective-permute-start | bytes 98312 | tf_op jit(solution)/shard_map/ppermute | solution.py:27
  8.2 3.7 %copy-start.4 = (s32[24,1]{0,1:T(1,128)S(1)}, s32[24,1]{0,1:T(1,128)}, u32[]{:S(2)}) copy-start(s32[24,1]{0,1:T(1,128)} %param.11) | copy-start | bytes 292
  9.1 4.0 %collective-permute-start.4 = (bf16[3,1,32,128]{3,2,1,0:T(8,128)(2,1)S(1)}, bf16[3,1,32,128]{3,2,1,0:T(8,128)(2,1)S(1)}, u32[]{:S(2)}, u32[]{:S(2)}) collective-permute-start(bf16[3,1,32,128]{3,2,1,0:T(8,128)(2,1)S(1)} %get-tuple-element.23), channel_id=1, source_target_pairs={{0,32},{32,64},{64,96},{96,0},{1,33},{33,65},{65,97},{97,1},{2,34}... | collective-permute-start | bytes 73736 | tf_op jit(solution)/shard_map/ppermute | solution.py:24
  9.9 3.2 collective-permute-start.5
  13.6 9.1 %collective-permute-start.6 = (bf16[3,194,1,128]{3,2,1,0:T(2,128)(2,1)S(1)}, bf16[3,194,1,128]{3,2,1,0:T(2,128)(2,1)S(1)}, u32[]{:S(2)}, u32[]{:S(2)}) collective-permute-start(bf16[3,194,1,128]{3,2,1,0:T(2,128)(2,1)S(1)} %get-tuple-element.21), channel_id=1, source_target_pairs={{0,1},{1,2},{2,3},{3,4},{4,5},{5,6},{6,7},{7,8},{8,9},{9,10},{10,1... | collective-permute-start | bytes 446984 | tf_op jit(solution)/shard_map/ppermute | solution.py:24
  17.4 6.5 %collective-permute-start.7 = (bf16[3,194,1,128]{3,2,1,0:T(2,128)(2,1)S(1)}, bf16[3,194,1,128]{3,2,1,0:T(2,128)(2,1)S(1)}, u32[]{:S(2)}, u32[]{:S(2)}) collective-permute-start(bf16[3,194,1,128]{3,2,1,0:T(2,128)(2,1)S(1)} %get-tuple-element.22), channel_id=1, source_target_pairs={{1,0},{2,1},{3,2},{4,3},{5,4},{6,5},{7,6},{8,7},{9,8},{10,9},{11,1... | collective-permute-start | bytes 446984 | tf_op jit(solution)/shard_map/ppermute | solution.py:27
  19.0 40.7 %collective-permute-start.2 = (bf16[4,194,1,128]{3,2,1,0:T(2,128)(2,1)S(1)}, bf16[4,194,1,128]{3,2,1,0:T(2,128)(2,1)S(1)}, u32[]{:S(2)}, u32[]{:S(2)}) collective-permute-start(bf16[4,194,1,128]{3,2,1,0:T(2,128)(2,1)S(1)} %get-tuple-element.17), channel_id=1, source_target_pairs={{0,1},{1,2},{2,3},{3,4},{4,5},{5,6},{6,7},{7,8},{8,9},{9,10},{10,1... | collective-permute-start | bytes 595976 | tf_op jit(solution)/shard_map/ppermute | solution.py:24
  20.7 38.9 %collective-permute-start.3 = (bf16[4,194,1,128]{3,2,1,0:T(2,128)(2,1)S(1)}, bf16[4,194,1,128]{3,2,1,0:T(2,128)(2,1)S(1)}, u32[]{:S(2)}, u32[]{:S(2)}) collective-permute-start(bf16[4,194,1,128]{3,2,1,0:T(2,128)(2,1)S(1)} %get-tuple-element.18), channel_id=1, source_target_pairs={{1,0},{2,1},{3,2},{4,3},{5,4},{6,5},{7,6},{8,7},{9,8},{10,9},{11,1... | collective-permute-start | bytes 595976 | tf_op jit(solution)/shard_map/ppermute | solution.py:27
  240.2 113.9 %all-to-all-start = ((bf16[32,2,32,1024]{3,2,1,0:T(8,128)(2,1)}), bf16[32,2,32,1024]{3,2,1,0:T(8,128)(2,1)}, u32[]{:S(2)}, u32[]{:S(2)}) async-start(bf16[32,2,32,1024]{3,2,1,0:T(8,128)(2,1)} %bitcast.61), calls=%async_computation | async-start | bytes 8388608 | tf_op jit(solution)/shard_map/all_to_all | solution.py:129
where the time goes:
time: 360 us; the launch traced here: 359 us
  other arithmetic  255 us (71%)
  local copies, waits for them, and re-layouts  78.5 us (22%)
  starting transfers between devices  22.4 us (6%)
    another operation x4, other arithmetic, flow_update(): return jnp.stack(result).astype(jnp.bfloat16)  104 us
    convert_element_type x1, other arithmetic, per_device(): charge.astype(jnp.bfloat16).reshape(BX, BLK, BLK, BZ, BLK)  86.4 us
    convert_element_type x1, other arithmetic, ion_update(): fields = padded.astype(jnp.float32)  32.1 us
    squeeze x1, local copies, waits for them, and re-layouts, ion_update(): density = fields[species]  22.4 us
    convert_element_type x1, other arithmetic, flow_update(): flow_field = flow_pad.astype(jnp.float32)  19.1 us
    squeeze x1, local copies, waits for them, and re-layouts, flow_update(): middle = [interior_view(flow_field[component]) for component in range(3)]  16.7 us
    convert_element_type x2, local copies, waits for them, and re-layouts, per_device(): charge.astype(jnp.bfloat16).reshape(BX, BLK, BLK, BZ, BLK)  15.7 us
    reshape x1, local copies, waits for them, and re-layouts, per_device(): charge_blocks = charge.astype(jnp.bfloat16).reshape(BX, BLK, BLK, BZ, BLK...  9.65 us
  transfers between devices with their start and end apart: 9, of which 2 were waited for; matrix products, arithmetic and copies ran while one was open for 40% of the time, Pallas kernels for 0%

commit v1 on v0

v1 whole, which is shorter than its diff:
```python
import functools

import jax
import jax.numpy as jnp
import numpy as np
from jax import lax
from jax.experimental import pallas as pl
from jax.experimental.pallas import tpu as pltpu
from jax.sharding import PartitionSpec as P

BLK = 32
BX = 6
BZ = 4
NXL = BX * BLK
NYL = BLK
NZL = BZ * BLK
ROWS = 48
LOW = 8
GROUP = 4

ion_step = 0.04
flow_step = 0.1
viscosity = 0.5
species_diff = (1.0, 1.5)

f32 = jnp.float32
bf16 = jnp.bfloat16


def near_sum_matrix():
    line = np.arange(NZL)
    return (np.abs(line[:, None] - line[None, :]) == 1).astype(np.float32)


def difference_matrix():
    line = np.arange(NZL)
    step = line[:, None] - line[None, :]
    return (step == 1).astype(np.float32) - (step == -1).astype(np.float32)


def block_order_matrix():
    order = np.zeros((4 * NZL, 4 * NZL), np.float32)
    for part in range(4):
        for block in range(BZ):
            for cell in range(BLK):
                order[part * NZL + block * BLK + cell, block * NZL + part * BLK + cell] = 1
    return order


def load_copies(pairs, sem, chunk):
    span = pl.ds(chunk * BLK, BLK)
    inner = pl.ds(chunk * BLK + 1, BLK)
    copies = []
    for number, (source, target, lead) in enumerate(pairs):
        index_from = (slice(None),) * lead + (span,)
        index_to = (slice(None),) * lead + (inner,)
        copies.append(
            pltpu.make_async_copy(source.at[index_from], target.at[index_to], sem.at[number, chunk])
        )
    return copies


def wait_chunks(step, pairs, sem):
    @pl.when(step == 0)
    def _():
        for copy in load_copies(pairs, sem, 0):
            copy.wait()

    @pl.when(step < BX - 1)
    def _():
        for copy in load_copies(pairs, sem, step + 1):
            copy.wait()


def ion_kernel(
    target_ref, filled_ref, conc_ref, pot_ref, diff_ref, spacer_ref, xlo_ref, xhi_ref,
    ylo_ref, yhi_ref, near_ref, order_ref,
    next_ref, out_ref,
    conc_in, pot_in, diff_in, spacer_in, wide, half, charge, lines, blocks, empty,
    load_sem, block_sem, empty_sem,
):
    step = pl.program_id(0)
    slots = filled_ref.shape[0]
    pairs = (
        (conc_ref, conc_in, 1),
        (pot_ref, pot_in, 0),
        (diff_ref, diff_in, 0),
        (spacer_ref, spacer_in, 0),
    )

    def empty_copy(slot):
        return pltpu.make_async_copy(empty, out_ref.at[slot], empty_sem.at[slot])

    def block_copy(chunk, part):
        return pltpu.make_async_copy(
            blocks.at[lax.rem(chunk, 2), part],
            out_ref.at[target_ref[chunk * BZ + part]],
            block_sem.at[lax.rem(chunk, 2), part],
        )

    @pl.when(step == 0)
    def _():
        for chunk in range(BX):
            for copy in load_copies(pairs, load_sem, chunk):
                copy.start()
        empty[...] = jnp.zeros_like(empty)

        @pl.loop(0, slots)
        def _(slot):
            @pl.when(filled_ref[slot] == 0)
            def _():
                empty_copy(slot).start()

        for plane, edge in ((0, xlo_ref), (NXL + 1, xhi_ref)):
            conc_in[0, plane] = edge[0]
            conc_in[1, plane] = edge[1]
            pot_in[plane] = edge[2]
            diff_in[plane] = edge[3]
            spacer_in[plane] = jnp.ones((NYL, NZL), jnp.int32)

    wait_chunks(step, pairs, load_sem)
    start = step * BLK

    def fields_of(first, second, pot, openness):
        root = openness * lax.rsqrt(jnp.maximum(openness, 1e-20))
        level = 0.5 * pot
        flux_first = root * first
        flux_second = root * second
        return (
            flux_first + level * flux_first,
            flux_first,
            flux_second - level * flux_second,
            flux_second,
            root,
            root * level,
        )

    @pl.loop(0, BLK + 2, unroll=2)
    def _(plane):
        at = start + plane
        openness = jnp.where(spacer_in[at] > 0, diff_in[at].astype(f32), 0.0)
        fields = fields_of(
            conc_in[0, at].astype(f32), conc_in[1, at].astype(f32), pot_in[at].astype(f32), openness
        )
        for number, field in enumerate(fields):
            wide[number, pl.ds(plane * ROWS + LOW, NYL), :] = field
            half[number, plane] = field.astype(bf16)

    for row, edge in ((LOW - 1, ylo_ref), (LOW + NYL, yhi_ref)):
        fields = fields_of(*[edge[number].astype(f32) for number in range(4)])
        for number, field in enumerate(fields):
            wide[number, pl.ds(ROWS + row, BLK, stride=ROWS), :] = field

    near = near_ref[...]

    @pl.loop(0, BLK // GROUP)
    def _(group):
        first = group * GROUP
        depth = []
        for number in range(6):
            centre = half[number, pl.ds(first + 1, GROUP)]
            sides = half[number, pl.ds(first, GROUP)] + half[number, pl.ds(first + 2, GROUP)]
            rows = jnp.concatenate([centre, sides], axis=2).reshape(GROUP * NYL, 2 * NZL)
            depth.append(jnp.dot(rows, near, preferred_element_type=f32))
        for plane in range(GROUP):
            base = (first + plane + 1) * ROWS + LOW
            total = []
            for number in range(6):
                total.append(
                    depth[number][plane * NYL : (plane + 1) * NYL]
                    + (
                        wide[number, pl.ds(base - 1, NYL), :]
                        + wide[number, pl.ds(base + 1, NYL), :]
                    )
                )
            at = start + first + plane + 1
            level = 0.5 * pot_in[at].astype(f32)
            root = ion_step * wide[4, pl.ds(base, NYL), :]
            tilt = level * total[4] - total[5]
            dens = conc_in[0, at].astype(f32)
            flux = total[0] - level * total[1] - dens * (total[4] + tilt)
            new_first = (dens + species_diff[0] * root * flux).astype(bf16)
            dens = conc_in[1, at].astype(f32)
            flux = total[2] + level * total[3] - dens * (total[4] - tilt)
            new_second = (dens + species_diff[1] * root * flux).astype(bf16)
            next_ref[0, first + plane] = new_first
            next_ref[1, first + plane] = new_second
            charge[pl.ds((first + plane) * NYL, NYL), :] = new_first.astype(f32) - new_second.astype(
                f32
            )

    for line in range(NYL // 4):
        for part in range(4):
            lines[pl.ds(line * BLK, BLK), pl.ds(part * NZL, NZL)] = charge[
                pl.ds(line * 4 + part, BLK, stride=NYL), :
            ].astype(bf16)

    @pl.when(step >= 2)
    def _():
        for part in range(BZ):
            block_copy(step - 2, part).wait()

    slot = lax.rem(step, 2)
    moved = jnp.dot(lines[...], order_ref[...], preferred_element_type=f32).astype(bf16)
    for line in range(NYL // 4):
        for part in range(BZ):
            blocks[slot, part, :, pl.ds(line * NZL, NZL)] = moved[
                line * BLK : (line + 1) * BLK, part * NZL : (part + 1) * NZL
            ]
    for part in range(BZ):
        block_copy(step, part).start()

    @pl.when(step == BX - 1)
    def _():
        for chunk in (BX - 2, BX - 1):
            for part in range(BZ):
                block_copy(chunk, part).wait()

        @pl.loop(0, slots)
        def _(slot):
            @pl.when(filled_ref[slot] == 0)
            def _():
                empty_copy(slot).wait()


def flow_kernel(
    vel_ref, pot_ref, spacer_ref, conc_ref, xlo_ref, xhi_ref, ylo_ref, yhi_ref, stencil_ref,
    out_ref,
    vel_in, pot_in, spacer_in, wide, half,
    load_sem,
):
    step = pl.program_id(0)
    pairs = ((vel_ref, vel_in, 1), (pot_ref, pot_in, 0), (spacer_ref, spacer_in, 0))

    @pl.when(step == 0)
    def _():
        for chunk in range(BX):
            for copy in load_copies(pairs, load_sem, chunk):
                copy.start()
        for plane, edge in ((0, xlo_ref), (NXL + 1, xhi_ref)):
            for number in range(3):
                vel_in[number, plane] = edge[number]
            pot_in[plane] = edge[3]
            spacer_in[plane] = jnp.ones((NYL, NZL), jnp.int32)

    wait_chunks(step, pairs, load_sem)
    start = step * BLK

    @pl.loop(0, BLK + 2, unroll=2)
    def _(plane):
        at = start + plane
        open_cells = spacer_in[at] > 0
        for number in range(3):
            field = jnp.where(open_cells, vel_in[number, at].astype(f32), 0.0)
            wide[number, pl.ds(plane * ROWS + LOW, NYL), :] = field
            half[number, plane] = field.astype(bf16)
        wide[3, pl.ds(plane * ROWS + LOW, NYL), :] = pot_in[at].astype(f32)

    for row, edge in ((LOW - 1, ylo_ref), (LOW + NYL, yhi_ref)):
        for number in range(4):
            wide[number, pl.ds(ROWS + row, BLK, stride=ROWS), :] = edge[number].astype(f32)

    stencil = stencil_ref[...]

    @pl.loop(0, BLK // GROUP)
    def _(group):
        first = group * GROUP
        depth = []
        for number in range(3):
            rows = half[number, pl.ds(first + 1, GROUP)].reshape(GROUP * NYL, NZL)
            depth.append(jnp.dot(rows, stencil, preferred_element_type=f32))
        rows = pot_in[pl.ds(start + first + 1, GROUP)].reshape(GROUP * NYL, NZL)
        pot_depth = jnp.dot(rows, stencil[:, NZL:], preferred_element_type=f32)
        for plane in range(GROUP):
            base = (first + plane + 1) * ROWS + LOW
            span = slice(plane * NYL, (plane + 1) * NYL)
            open_cells = spacer_in[start + first + plane + 1] > 0

            def near(number, offset):
                return wide[number, pl.ds(base + offset, NYL), :]

            charge = conc_ref[0, first + plane].astype(f32) - conc_ref[1, first + plane].astype(f32)
            centre = [near(number, 0) for number in range(3)]
            slopes = (
                near(3, ROWS) - near(3, -ROWS),
                near(3, 1) - near(3, -1),
                pot_depth[span],
            )
            for number in range(3):
                front, back = near(number, ROWS), near(number, -ROWS)
                right, left = near(number, 1), near(number, -1)
                total = (front + back) + (right + left) + depth[number][span, :NZL]
                carried = (
                    centre[0] * (front - back)
                    + centre[1] * (right - left)
                    + centre[2] * depth[number][span, NZL:]
                )
                value = (1.0 - 6.0 * flow_step * viscosity) * centre[number] + (
                    flow_step * viscosity
                ) * total - (0.5 * flow_step) * (carried + charge * slopes[number])
                out_ref[number, first + plane] = jnp.where(open_cells, value, 0.0).astype(bf16)


def any_spec():
    return pl.BlockSpec(memory_space=pl.ANY)


def whole_spec(shape):
    return pl.BlockSpec(shape, lambda step: (0,) * len(shape))


def run_ions(target, filled, concentration, potential, diffusivity, spacer, xlo, xhi, ylo, yhi):
    near = jnp.asarray(np.concatenate([near_sum_matrix(), np.eye(NZL, dtype=np.float32)]), bf16)
    order = jnp.asarray(block_order_matrix(), bf16)
    slots = filled.shape[0]
    plane = (NXL + 2, NYL, NZL)
    edge = pl.BlockSpec((4, BLK, NZL), lambda step: (0, step, 0))
    return pl.pallas_call(
        ion_kernel,
        grid=(BX,),
        in_specs=[
            pl.BlockSpec(memory_space=pltpu.SMEM),
            pl.BlockSpec(memory_space=pltpu.SMEM),
            any_spec(), any_spec(), any_spec(), any_spec(),
            whole_spec(xlo.shape), whole_spec(xhi.shape), edge, edge,
            whole_spec(near.shape), whole_spec(order.shape),
        ],
        out_specs=[
            pl.BlockSpec((2, BLK, NYL, NZL), lambda step: (0, step, 0, 0)),
            any_spec(),
        ],
        out_shape=[
            jax.ShapeDtypeStruct(concentration.shape, bf16),
            jax.ShapeDtypeStruct((slots, BLK, BLK * BLK), bf16),
        ],
        scratch_shapes=[
            pltpu.VMEM((2,) + plane, bf16),
            pltpu.VMEM(plane, bf16),
            pltpu.VMEM(plane, bf16),
            pltpu.VMEM(plane, jnp.int32),
            pltpu.VMEM((6, (BLK + 2) * ROWS, NZL), f32),
            pltpu.VMEM((6, BLK + 2, NYL, NZL), bf16),
            pltpu.VMEM((BLK * NYL, NZL), f32),
            pltpu.VMEM((NYL // 4 * BLK, 4 * NZL), bf16),
            pltpu.VMEM((2, BZ, BLK, BLK * BLK), bf16),
            pltpu.VMEM((BLK, BLK * BLK), bf16),
            pltpu.SemaphoreType.DMA((4, BX)),
            pltpu.SemaphoreType.DMA((2, BZ)),
            pltpu.SemaphoreType.DMA((slots,)),
        ],
        compiler_params=pltpu.CompilerParams(vmem_limit_bytes=48 * 1024 * 1024),
        cost_estimate=pl.CostEstimate(flops=200_000_000, bytes_accessed=17_000_000, transcendentals=0),
        name="ions",
    )(target, filled, concentration, potential, diffusivity, spacer, xlo, xhi, ylo, yhi, near, order)


def run_flow(velocity, potential, spacer, conc_next, xlo, xhi, ylo, yhi):
    stencil = jnp.asarray(np.concatenate([near_sum_matrix(), difference_matrix()], axis=1), bf16)
    plane = (NXL + 2, NYL, NZL)
    edge = pl.BlockSpec((4, BLK, NZL), lambda step: (0, step, 0))
    return pl.pallas_call(
        flow_kernel,
        grid=(BX,),
        in_specs=[
            any_spec(), any_spec(), any_spec(),
            pl.BlockSpec((2, BLK, NYL, NZL), lambda step: (0, step, 0, 0)),
            whole_spec(xlo.shape), whole_spec(xhi.shape), edge, edge,
            whole_spec(stencil.shape),
        ],
        out_specs=pl.BlockSpec((3, BLK, NYL, NZL), lambda step: (0, step, 0, 0)),
        out_shape=jax.ShapeDtypeStruct(velocity.shape, bf16),
        scratch_shapes=[
            pltpu.VMEM((3,) + plane, bf16),
            pltpu.VMEM(plane, bf16),
            pltpu.VMEM(plane, jnp.int32),
            pltpu.VMEM((4, (BLK + 2) * ROWS, NZL), f32),
            pltpu.VMEM((3, BLK + 2, NYL, NZL), bf16),
            pltpu.SemaphoreType.DMA((3, BX)),
        ],
        compiler_params=pltpu.CompilerParams(vmem_limit_bytes=48 * 1024 * 1024),
        cost_estimate=pl.CostEstimate(flops=200_000_000, bytes_accessed=17_000_000, transcendentals=0),
        name="flow",
    )(velocity, potential, spacer, conc_next, xlo, xhi, ylo, yhi, stencil)


def exchange(low_edge, high_edge, axis):
    count = lax.axis_size(axis)
    forward = [(i, (i + 1) % count) for i in range(count)]
    backward = [(i, (i - 1) % count) for i in range(count)]
    return lax.ppermute(high_edge, axis, forward), lax.ppermute(low_edge, axis, backward)


def per_device(concentration, potential, diffusivity, spacer, velocity, balance_plan):
    tiles = lax.axis_size("tile")
    count = balance_plan.shape[0]
    capacity = max(2, (2 * count + tiles - 1) // tiles)
    slots = tiles * capacity

    def cut(array, dim, index):
        return lax.index_in_dim(array, index, dim, keepdims=False)

    def edges_of(dim, index):
        solid = cut(spacer, dim, index) > 0
        conc = cut(concentration, dim + 1, index)
        pot = cut(potential, dim, index)[None]
        openness = jnp.where(solid, cut(diffusivity, dim, index), 0)[None]
        moving = jnp.where(solid[None], cut(velocity, dim + 1, index), 0)
        return jnp.concatenate([conc, pot, openness.astype(bf16)]), moving.astype(bf16)

    x_ion_low, x_flow_low = edges_of(0, 0)
    x_ion_high, x_flow_high = edges_of(0, NXL - 1)
    y_ion_low, y_flow_low = edges_of(1, 0)
    y_ion_high, y_flow_high = edges_of(1, NYL - 1)
    xlo, xhi = exchange(x_ion_low, x_ion_high, "stream")
    ylo, yhi = exchange(y_ion_low, y_ion_high, "tile")
    flow_xlo, flow_xhi = exchange(x_flow_low, x_flow_high, "stream")
    flow_ylo, flow_yhi = exchange(y_flow_low, y_flow_high, "tile")

    owners = balance_plan[:, 0]
    number = jnp.arange(count, dtype=jnp.int32)
    same_owner = owners[:, None] == owners[None, :]
    earlier = number[:, None] < number[None, :]
    ranking = jnp.sum(jnp.logical_and(same_owner, earlier).astype(jnp.int32), axis=0)
    target = owners * capacity + ranking
    filled = jnp.sum(
        (target[None, :] == jnp.arange(slots, dtype=jnp.int32)[:, None]).astype(jnp.int32), axis=1
    )

    conc_next, outgoing = run_ions(
        target, filled, concentration, potential, diffusivity, spacer, xlo, xhi, ylo, yhi
    )
    outgoing = outgoing.reshape(tiles, capacity, BLK, BLK * BLK)
    owned = lax.all_to_all(outgoing, "tile", split_axis=0, concat_axis=0, tiled=True)
    owned = owned.reshape(slots, BLK, BLK * BLK)

    def with_pot(flow, ion):
        return jnp.concatenate([flow, ion[2:3]])

    flow_next = run_flow(
        velocity, potential, spacer, conc_next,
        with_pot(flow_xlo, xlo), with_pot(flow_xhi, xhi),
        with_pot(flow_ylo, ylo), with_pot(flow_yhi, yhi),
    )
    return (conc_next, flow_next, owned)


def solution(mesh):
    placed = (
        P(None, "stream", "tile", None),
        P("stream", "tile", None),
        P("stream", "tile", None),
        P("stream", "tile", None),
        P(None, "stream", "tile", None),
        P(("stream", "tile"), None),
    )
    return jax.shard_map(
        per_device,
        mesh=mesh,
        in_specs=placed,
        out_specs=(
            P(None, "stream", "tile", None),
            P(None, "stream", "tile", None),
            P(("stream", "tile"), None, None),
        ),
        check_vma=False,
    )
```

time: 360 us -> 130 us (0.36)
  other arithmetic: 255 us -> 2.34 us
  local copies, waits for them, and re-layouts: 78.5 us -> 13.9 us
  waiting for transfers between devices: 2.3 us -> 49.3 us
  Pallas kernels: 0 us -> 44.1 us
  starting transfers between devices: 22.4 us -> 18.6 us
    convert_element_type x4 -> x0, other arithmetic: 143 us -> none  [the longest x1 86.4 us: per_device(): charge.astype(jnp.bfloat16).reshape(BX, BLK, BLK, BZ, BLK)]
    another operation x5 -> x0, other arithmetic: 106 us -> none  [the longest x4 104 us: flow_update(): return jnp.stack(result).astype(jnp.bfloat16)]
    ppermute x8, waiting for transfers between devices: 2.29 us -> 49.3 us  [the longest x4 44.7 us: exchange(): lax.ppermute(high_edge, axis, forward)]
    pallas_call x0 -> x2, Pallas kernels: none -> 44.1 us  [the longest x1 27.1 us: run_ions(): pl.pallas_call(ion_kernel, grid=(BX,), in_specs=[pl.BlockSpec(memory_spac...]
    squeeze x2 -> x1, local copies, waits for them, and re-layouts: 39 us -> 0.89 us  [cut(): return lax.index_in_dim(array, index, dim, keepdims=False)]
    convert_element_type x2 -> x0, local copies, waits for them, and re-layouts: 15.7 us -> none  [per_device(): charge.astype(jnp.bfloat16).reshape(BX, BLK, BLK, BZ, BLK)]
    reshape x1 -> x0, local copies, waits for them, and re-layouts: 9.65 us -> none  [per_device(): charge_blocks = charge.astype(jnp.bfloat16).reshape(BX, BLK, BLK, BZ, BLK...]
    slice x1 -> x9, local copies, waits for them, and re-layouts: 0.01 us -> 7.9 us  [the longest x5 7.88 us: cut(): return lax.index_in_dim(array, index, dim, keepdims=False)]
  transfers between devices with their start and end apart: 9 -> 9, of which waited for: 2 -> 4; matrix products, arithmetic and copies ran while one was open for 40% -> 7% of each run, Pallas kernels for 0% -> 13%
where the time goes in v1:
time: 130 us; the launch traced here: 129 us
  waiting for transfers between devices  49.3 us (38%)
  Pallas kernels  44.1 us (34%)
  starting transfers between devices  18.6 us (14%)
  local copies, waits for them, and re-layouts  13.9 us (11%)
  other arithmetic  2.34 us (2%)
    ppermute x4, waiting for transfers between devices, exchange(): lax.ppermute(high_edge, axis, forward)  44.7 us
    pallas_call x1, Pallas kernels, run_ions(): pl.pallas_call(ion_kernel, grid=(BX,), in_specs=[pl.BlockSpec(memory_spac...  27.1 us
    pallas_call x1, Pallas kernels, run_flow(): pl.pallas_call(flow_kernel, grid=(BX,), in_specs=[any_spec(), any_spec(),...  16.9 us
    all_to_all x1, starting transfers between devices, per_device(): lax.all_to_all(outgoing, 'tile', split_axis=0, concat_axis=0, tiled=True)  8.27 us
    slice x5, local copies, waits for them, and re-layouts, cut(): return lax.index_in_dim(array, index, dim, keepdims=False)  7.88 us
    ppermute x4, starting transfers between devices, exchange(): lax.ppermute(high_edge, axis, forward)  7.25 us
    unnamed x19, local copies, waits for them, and re-layouts  5.1 us
    ppermute x4, waiting for transfers between devices, exchange(): lax.ppermute(low_edge, axis, backward)  4.59 us
  transfers between devices with their start and end apart: 9, of which 4 were waited for; matrix products, arithmetic and copies ran while one was open for 7% of the time, Pallas kernels for 13%

profile of v1, /device:TPU:1, one launch (start us, length us, event | category | flops | bytes accessed | tf_op | source)
XLA Modules:
  0.0 129.1 jit_solution(14218288011433634216)
XLA Ops:
  0.6 0.0 copy-start.3
  0.6 0.0 copy-start.5
  0.7 0.0 copy-start.1
  0.7 0.9 slice_bitcast_fusion
  1.6 1.0 slice_select_fusion
  2.6 2.2 %collective-permute-start = (bf16[4,32,128]{2,1,0:T(8,128)(2,1)S(1)}, bf16[4,32,128]{2,1,0:T(8,128)(2,1)S(1)}, u32[]{:S(2)}, u32[]{:S(2)}) collective-permute-start(bf16[4,32,128]{2,1,0:T(8,128)(2,1)S(1)} %pad_maximum_fusion.4), channel_id=1, source_target_pairs={{0,32},{32,64},{64,96},{96,0},{1,33},{33,65},{65,97},{97,1},{2,34}... | collective-permute-start | bytes 98312 | tf_op jit(solution)/shard_map/ppermute | solution.py:390
  4.8 1.5 %collective-permute-start.1 = (bf16[4,32,128]{2,1,0:T(8,128)(2,1)S(1)}, bf16[4,32,128]{2,1,0:T(8,128)(2,1)S(1)}, u32[]{:S(2)}, u32[]{:S(2)}) collective-permute-start(bf16[4,32,128]{2,1,0:T(8,128)(2,1)S(1)} %pad_maximum_fusion.5), channel_id=1, source_target_pairs={{0,96},{32,0},{64,32},{96,64},{1,97},{33,1},{65,33},{97,65},{2,98}... | collective-permute-start | bytes 98312 | tf_op jit(solution)/shard_map/ppermute | solution.py:390
  6.3 1.3 fusion.9
  7.6 1.3 fusion.8
  8.9 1.5 %fusion.7 = (s32[192,1,128]{2,1,0:T(1,128)S(1)}, s32[192,1,128]{2,1,0:T(1,128)S(1)}) fusion(s32[192,32,128]{2,1,0:T(8,128)} %spacer_ref.3), kind=kLoop, calls=%fused_computation.38 | loop fusion | bytes 393216 | tf_op jit(solution)/shard_map/slice | solution.py:400
  10.4 1.7 %fusion.6 = (bf16[2,192,1,128]{3,2,1,0:T(2,128)(2,1)S(1)}, bf16[2,192,1,128]{3,2,1,0:T(2,128)(2,1)S(1)}) fusion(bf16[2,192,32,128]{3,2,1,0:T(8,128)(2,1)} %conc_ref.1), kind=kLoop, calls=%fused_computation.37 | loop fusion | bytes 393216 | tf_op jit(solution)/shard_map/slice | solution.py:400
  12.2 0.1 fusion.2
  12.3 2.7 %collective-permute-start.2 = (bf16[4,192,128]{2,1,0:T(8,128)(2,1)S(1)}, bf16[4,192,128]{2,1,0:T(8,128)(2,1)S(1)}, u32[]{:S(2)}, u32[]{:S(2)}) collective-permute-start(bf16[4,192,128]{2,1,0:T(8,128)(2,1)S(1)} %pad_maximum_fusion), channel_id=1, source_target_pairs={{0,1},{1,2},{2,3},{3,4},{4,5},{5,6},{6,7},{7,8},{8,9},{9,10},{10,1... | collective-permute-start | bytes 589832 | tf_op jit(solution)/shard_map/ppermute | solution.py:390
  15.0 0.1 collective-permute-start.3
  15.1 0.1 convert_reduce_fusion.1
  15.2 0.1 convert_reduce_fusion.filled_ref
  15.3 2.2 %collective-permute-done.2.ylo_ref = bf16[4,192,128]{2,1,0:T(8,128)(2,1)S(1)} collective-permute-done((bf16[4,192,128]{2,1,0:T(8,128)(2,1)S(1)}, bf16[4,192,128]{2,1,0:T(8,128)(2,1)S(1)}, u32[]{:S(2)}, u32[]{:S(2)}) %collective-permute-start.2) | collective-permute-done | bytes 196640 | tf_op jit(solution)/shard_map/ppermute | solution.py:390
  17.6 2.9 %collective-permute-done.3.yhi_ref = bf16[4,192,128]{2,1,0:T(8,128)(2,1)S(1)} collective-permute-done((bf16[4,192,128]{2,1,0:T(8,128)(2,1)S(1)}, bf16[4,192,128]{2,1,0:T(8,128)(2,1)S(1)}, u32[]{:S(2)}, u32[]{:S(2)}) %collective-permute-start.3) | collective-permute-done | bytes 196640 | tf_op jit(solution)/shard_map/ppermute | solution.py:390
  20.5 27.1 %ions.1 = (bf16[2,192,32,128]{3,2,1,0:T(8,128)(2,1)}, bf16[64,32,1024]{2,1,0:T(8,128)(2,1)}) custom-call(s32[24]{0:T(128)S(1)} %multiply_add_fusion.target_ref, s32[64]{0:T(128)S(1)} %convert_reduce_fusion.filled_ref, bf16[2,192,32,128]{3,2,1,0:T(8,128)(2,1)} %conc_ref.1, bf16[192,32,128]{2,1,0:T(8,128)(2,1)S(1)} %copy-done.1, ...), custom_call_target="tpu_custom_call" | custom-call | flops 200000000 | bytes 17000000 | tf_op jit(solution)/shard_map/ions/pallas_call | solution.py:318
  47.6 8.3 %all-to-all-start = ((bf16[32,2,32,1024]{3,2,1,0:T(8,128)(2,1)}), bf16[32,2,32,1024]{3,2,1,0:T(8,128)(2,1)}, u32[]{:S(2)}, u32[]{:S(2)}) async-start(bf16[32,2,32,1024]{3,2,1,0:T(8,128)(2,1)} %bitcast.50), calls=%async_computation | async-start | bytes 8388608 | tf_op jit(solution)/shard_map/all_to_all | solution.py:433
  55.9 0.0 copy-start
  55.9 0.0 copy-start.4
  55.9 0.9 bitcast_select_fusion
  56.9 1.4 %collective-permute-start.5 = (bf16[3,32,128]{2,1,0:T(8,128)(2,1)S(1)}, bf16[3,32,128]{2,1,0:T(8,128)(2,1)S(1)}, u32[]{:S(2)}, u32[]{:S(2)}) collective-permute-start(bf16[3,32,128]{2,1,0:T(8,128)(2,1)S(1)} %get-tuple-element.17), channel_id=1, source_target_pairs={{0,96},{32,0},{64,32},{96,64},{1,97},{33,1},{65,33},{97,65},{2,98}... | collective-permute-start | bytes 73736 | tf_op jit(solution)/shard_map/ppermute | solution.py:390
  58.2 0.1 collective-permute-start.4
  58.3 2.1 %fusion.5 = (bf16[3,192,1,128]{3,2,1,0:T(2,128)(2,1)S(1)}, bf16[3,192,1,128]{3,2,1,0:T(2,128)(2,1)S(1)}) fusion(bf16[3,192,32,128]{3,2,1,0:T(8,128)(2,1)} %vel_ref.1), kind=kLoop, calls=%fused_computation.36 | loop fusion | bytes 589824 | tf_op jit(solution)/shard_map/slice | solution.py:400
  60.5 2.3 %collective-permute-start.6 = (bf16[3,192,128]{2,1,0:T(8,128)(2,1)S(1)}, bf16[3,192,128]{2,1,0:T(8,128)(2,1)S(1)}, u32[]{:S(2)}, u32[]{:S(2)}) collective-permute-start(bf16[3,192,128]{2,1,0:T(8,128)(2,1)S(1)} %fusion.1), channel_id=1, source_target_pairs={{0,1},{1,2},{2,3},{3,4},{4,5},{5,6},{6,7},{7,8},{8,9},{9,10},{10,1... | collective-permute-start | bytes 442376 | tf_op jit(solution)/shard_map/ppermute | solution.py:390
  62.8 0.1 collective-permute-start.7
  62.9 42.5 %collective-permute-done.6 = bf16[3,192,128]{2,1,0:T(8,128)(2,1)S(1)} collective-permute-done((bf16[3,192,128]{2,1,0:T(8,128)(2,1)S(1)}, bf16[3,192,128]{2,1,0:T(8,128)(2,1)S(1)}, u32[]{:S(2)}, u32[]{:S(2)}) %collective-permute-start.6) | collective-permute-done | bytes 147488 | tf_op jit(solution)/shard_map/ppermute | solution.py:390
  105.4 1.7 %collective-permute-done.7 = bf16[3,192,128]{2,1,0:T(8,128)(2,1)S(1)} collective-permute-done((bf16[3,192,128]{2,1,0:T(8,128)(2,1)S(1)}, bf16[3,192,128]{2,1,0:T(8,128)(2,1)S(1)}, u32[]{:S(2)}, u32[]{:S(2)}) %collective-permute-start.7) | collective-permute-done | bytes 147488 | tf_op jit(solution)/shard_map/ppermute | solution.py:390
  107.2 16.9 %flow.1 = bf16[3,192,32,128]{3,2,1,0:T(8,128)(2,1)} custom-call(bf16[3,192,32,128]{3,2,1,0:T(8,128)(2,1)} %vel_ref.1, bf16[192,32,128]{2,1,0:T(8,128)(2,1)S(1)} %copy-done.1, s32[192,32,128]{2,1,0:T(8,128)S(1)} %copy-done, bf16[2,192,32,128]{3,2,1,0:T(8,128)(2,1)} %get-tuple-element.40.conc_ref, bf16[4,32,128]{2,1,0:T(8,128)(2,1)S(1)} %pad_maximum_fusion.6.xlo_ref, ...), custom_call_target="tpu_custom_call" | custom-call | flops 200000000 | bytes 17000000 | tf_op jit(solution)/shard_map/flow/pallas_call | solution.py:361
  124.1 5.0 %copy.75 = bf16[64,32,1024]{2,1,0:T(8,128)(2,1)} copy(bf16[64,32,1024]{2,1,0:T(8,128)(2,1)} %bitcast.18) | data formatting | bytes 8388608
  (33 shorter events, 0.3 us)
Async XLA Ops:
  0.6 19.9 %copy-start.3 = (bf16[512,512]{1,0:T(8,128)(2,1)S(1)}, bf16[512,512]{1,0:T(8,128)(2,1)}, u32[]{:S(2)}) copy-start(bf16[512,512]{1,0:T(8,128)(2,1)} %constant.15.clone.order_ref) | copy-start | bytes 1572868
  0.6 19.9 %copy-start.5 = (bf16[256,128]{1,0:T(8,128)(2,1)S(1)}, bf16[256,128]{1,0:T(8,128)(2,1)}, u32[]{:S(2)}) copy-start(bf16[256,128]{1,0:T(8,128)(2,1)} %constant.14.clone.near_ref) | copy-start | bytes 196612
  0.7 19.8 %copy-start.1 = (bf16[192,32,128]{2,1,0:T(8,128)(2,1)S(1)}, bf16[192,32,128]{2,1,0:T(8,128)(2,1)}, u32[]{:S(2)}) copy-start(bf16[192,32,128]{2,1,0:T(8,128)(2,1)} %pot_ref.3) | copy-start | bytes 4718596
  0.7 19.8 %copy-start.2 = (bf16[192,32,128]{2,1,0:T(8,128)(2,1)S(1)}, bf16[192,32,128]{2,1,0:T(8,128)(2,1)}, u32[]{:S(2)}) copy-start(bf16[192,32,128]{2,1,0:T(8,128)(2,1)} %diff_ref.1) | copy-start | bytes 4718596
  0.7 14.4 %copy-start.6 = (s32[24,1]{0,1:T(1,128)S(1)}, s32[24,1]{0,1:T(1,128)}, u32[]{:S(2)}) copy-start(s32[24,1]{0,1:T(1,128)} %param.14) | copy-start | bytes 292
  2.6 12.7 %collective-permute-start = (bf16[4,32,128]{2,1,0:T(8,128)(2,1)S(1)}, bf16[4,32,128]{2,1,0:T(8,128)(2,1)S(1)}, u32[]{:S(2)}, u32[]{:S(2)}) collective-permute-start(bf16[4,32,128]{2,1,0:T(8,128)(2,1)S(1)} %pad_maximum_fusion.4), channel_id=1, source_target_pairs={{0,32},{32,64},{64,96},{96,0},{1,33},{33,65},{65,97},{97,1},{2,34}... | collective-permute-start | bytes 98312 | tf_op jit(solution)/shard_map/ppermute | solution.py:390
  4.8 10.5 %collective-permute-start.1 = (bf16[4,32,128]{2,1,0:T(8,128)(2,1)S(1)}, bf16[4,32,128]{2,1,0:T(8,128)(2,1)S(1)}, u32[]{:S(2)}, u32[]{:S(2)}) collective-permute-start(bf16[4,32,128]{2,1,0:T(8,128)(2,1)S(1)} %pad_maximum_fusion.5), channel_id=1, source_target_pairs={{0,96},{32,0},{64,32},{96,64},{1,97},{33,1},{65,33},{97,65},{2,98}... | collective-permute-start | bytes 98312 | tf_op jit(solution)/shard_map/ppermute | solution.py:390
  12.3 5.3 %collective-permute-start.2 = (bf16[4,192,128]{2,1,0:T(8,128)(2,1)S(1)}, bf16[4,192,128]{2,1,0:T(8,128)(2,1)S(1)}, u32[]{:S(2)}, u32[]{:S(2)}) collective-permute-start(bf16[4,192,128]{2,1,0:T(8,128)(2,1)S(1)} %pad_maximum_fusion), channel_id=1, source_target_pairs={{0,1},{1,2},{2,3},{3,4},{4,5},{5,6},{6,7},{7,8},{8,9},{9,10},{10,1... | collective-permute-start | bytes 589832 | tf_op jit(solution)/shard_map/ppermute | solution.py:390
  15.0 5.5 %collective-permute-start.3 = (bf16[4,192,128]{2,1,0:T(8,128)(2,1)S(1)}, bf16[4,192,128]{2,1,0:T(8,128)(2,1)S(1)}, u32[]{:S(2)}, u32[]{:S(2)}) collective-permute-start(bf16[4,192,128]{2,1,0:T(8,128)(2,1)S(1)} %pad_maximum_fusion.1), channel_id=1, source_target_pairs={{0,31},{1,0},{2,1},{3,2},{4,3},{5,4},{6,5},{7,6},{8,7},{9,8},{10,9... | collective-permute-start | bytes 589832 | tf_op jit(solution)/shard_map/ppermute | solution.py:390
  47.6 76.5 %all-to-all-start = ((bf16[32,2,32,1024]{3,2,1,0:T(8,128)(2,1)}), bf16[32,2,32,1024]{3,2,1,0:T(8,128)(2,1)}, u32[]{:S(2)}, u32[]{:S(2)}) async-start(bf16[32,2,32,1024]{3,2,1,0:T(8,128)(2,1)} %bitcast.50), calls=%async_computation | async-start | bytes 8388608 | tf_op jit(solution)/shard_map/all_to_all | solution.py:433
  55.9 51.2 %copy-start = (s32[192,32,128]{2,1,0:T(8,128)S(1)}, s32[192,32,128]{2,1,0:T(8,128)}, u32[]{:S(2)}) copy-start(s32[192,32,128]{2,1,0:T(8,128)} %spacer_ref.3) | copy-start | bytes 9437188
  55.9 51.2 %copy-start.4 = (bf16[128,256]{1,0:T(8,128)(2,1)S(1)}, bf16[128,256]{1,0:T(8,128)(2,1)}, u32[]{:S(2)}) copy-start(bf16[128,256]{1,0:T(8,128)(2,1)} %constant.16.clone.stencil_ref) | copy-start | bytes 196612
  56.9 6.0 %collective-permute-start.5 = (bf16[3,32,128]{2,1,0:T(8,128)(2,1)S(1)}, bf16[3,32,128]{2,1,0:T(8,128)(2,1)S(1)}, u32[]{:S(2)}, u32[]{:S(2)}) collective-permute-start(bf16[3,32,128]{2,1,0:T(8,128)(2,1)S(1)} %get-tuple-element.17), channel_id=1, source_target_pairs={{0,96},{32,0},{64,32},{96,64},{1,97},{33,1},{65,33},{97,65},{2,98}... | collective-permute-start | bytes 73736 | tf_op jit(solution)/shard_map/ppermute | solution.py:390
  58.2 4.6 %collective-permute-start.4 = (bf16[3,32,128]{2,1,0:T(8,128)(2,1)S(1)}, bf16[3,32,128]{2,1,0:T(8,128)(2,1)S(1)}, u32[]{:S(2)}, u32[]{:S(2)}) collective-permute-start(bf16[3,32,128]{2,1,0:T(8,128)(2,1)S(1)} %get-tuple-element.18), channel_id=1, source_target_pairs={{0,32},{32,64},{64,96},{96,0},{1,33},{33,65},{65,97},{97,1},{2,34}... | collective-permute-start | bytes 73736 | tf_op jit(solution)/shard_map/ppermute | solution.py:390
  60.5 45.0 %collective-permute-start.6 = (bf16[3,192,128]{2,1,0:T(8,128)(2,1)S(1)}, bf16[3,192,128]{2,1,0:T(8,128)(2,1)S(1)}, u32[]{:S(2)}, u32[]{:S(2)}) collective-permute-start(bf16[3,192,128]{2,1,0:T(8,128)(2,1)S(1)} %fusion.1), channel_id=1, source_target_pairs={{0,1},{1,2},{2,3},{3,4},{4,5},{5,6},{6,7},{7,8},{8,9},{9,10},{10,1... | collective-permute-start | bytes 442376 | tf_op jit(solution)/shard_map/ppermute | solution.py:390
  62.8 44.4 %collective-permute-start.7 = (bf16[3,192,128]{2,1,0:T(8,128)(2,1)S(1)}, bf16[3,192,128]{2,1,0:T(8,128)(2,1)S(1)}, u32[]{:S(2)}, u32[]{:S(2)}) collective-permute-start(bf16[3,192,128]{2,1,0:T(8,128)(2,1)S(1)} %fusion), channel_id=1, source_target_pairs={{0,31},{1,0},{2,1},{3,2},{4,3},{5,4},{6,5},{7,6},{8,7},{9,8},{10,9... | collective-permute-start | bytes 442376 | tf_op jit(solution)/shard_map/ppermute | solution.py:390

commit v2 on v1

v2 whole, which is shorter than its diff:
```python
import jax
import jax.numpy as jnp
import numpy as np
from jax import lax
from jax.experimental import pallas as pl
from jax.experimental.pallas import tpu as pltpu
from jax.sharding import PartitionSpec as P

BLK = 32
BX = 6
BZ = 4
NXL = BX * BLK
NYL = BLK
NZL = BZ * BLK
ROWS = 48
LOW = 8
GROUP = 8
PART = 8

MESH = pl.DeviceIdType.MESH

ion_step = 0.04
flow_step = 0.1
viscosity = 0.5
species_diff = (1.0, 1.5)

f32 = jnp.float32
bf16 = jnp.bfloat16


def near_sum_matrix():
    line = np.arange(NZL)
    return (np.abs(line[:, None] - line[None, :]) == 1).astype(np.float32)


def difference_matrix():
    line = np.arange(NZL)
    step = line[:, None] - line[None, :]
    return (step == 1).astype(np.float32) - (step == -1).astype(np.float32)


def block_order_matrix():
    order = np.zeros((4 * NZL, 4 * NZL), np.float32)
    for part in range(4):
        for block in range(BZ):
            for cell in range(BLK):
                order[part * NZL + block * BLK + cell, block * NZL + part * BLK + cell] = 1
    return order


def load_copies(pairs, sem, chunk):
    span = pl.ds(chunk * BLK, BLK)
    inner = pl.ds(chunk * BLK + 1, BLK)
    copies = []
    for number, (source, target, lead) in enumerate(pairs):
        index_from = (slice(None),) * lead + (span,)
        index_to = (slice(None),) * lead + (inner,)
        copies.append(
            pltpu.make_async_copy(source.at[index_from], target.at[index_to], sem.at[number, chunk])
        )
    return copies


def wait_chunks(step, pairs, sem):
    @pl.when(step == 0)
    def _():
        for copy in load_copies(pairs, sem, 0):
            copy.wait()

    @pl.when(step < BX - 1)
    def _():
        for copy in load_copies(pairs, sem, step + 1):
            copy.wait()


def ion_kernel(
    source_ref, conc_ref, pot_ref, diff_ref, spacer_ref, vel_ref, near_ref, order_ref,
    next_ref, out_ref, yhalo_ref, xhalo_ref,
    conc_in, pot_in, diff_in, spacer_in, vel_in, vel_edge, edge_rows, y_send, y_recv, x_out,
    wide, half, charge, lines, blocks, staged, fresh,
    load_sem, vel_sem, xs_sem, xr_sem, ys_sem, yr_sem, fresh_sem, out_sem, halo_sem,
):
    slots = out_ref.shape[0]
    stream, tile = lax.axis_index("stream"), lax.axis_index("tile")
    streams, tiles = lax.axis_size("stream"), lax.axis_size("tile")
    x_near = (lax.rem(stream + streams - 1, streams), lax.rem(stream + 1, streams))
    y_near = (lax.rem(tile + tiles - 1, tiles), lax.rem(tile + 1, tiles))
    pairs = (
        (conc_ref, conc_in, 1),
        (pot_ref, pot_in, 0),
        (diff_ref, diff_in, 0),
        (spacer_ref, spacer_in, 0),
    )

    def vel_copy(chunk):
        span = pl.ds(chunk * BLK, BLK)
        return pltpu.make_async_copy(vel_ref.at[:, span], vel_in.at[:, span], vel_sem.at[chunk])

    def x_copies(side):
        edge = (0, NXL - 1)[side]
        halo = (NXL + 1, 0)[side]
        ends = (
            (conc_ref.at[:, edge], conc_in.at[:, halo]),
            (pot_ref.at[edge], pot_in.at[halo]),
            (diff_ref.at[edge], diff_in.at[halo]),
            (spacer_ref.at[edge], spacer_in.at[halo]),
            (vel_ref.at[:, edge], vel_edge.at[1 - side]),
        )
        return [
            pltpu.make_async_remote_copy(
                src_ref=source,
                dst_ref=target,
                send_sem=xs_sem.at[side, number],
                recv_sem=xr_sem.at[side, number],
                device_id=(x_near[side], tile),
                device_id_type=MESH,
            )
            for number, (source, target) in enumerate(ends)
        ]

    def y_copy(side, chunk):
        span = pl.ds(chunk * BLK, BLK)
        return pltpu.make_async_remote_copy(
            src_ref=y_send.at[side, :, span],
            dst_ref=y_recv.at[1 - side, :, span],
            send_sem=ys_sem.at[side, chunk],
            recv_sem=yr_sem.at[side, chunk],
            device_id=(stream, y_near[side]),
            device_id_type=MESH,
        )

    def fresh_copy(chunk):
        slot = lax.rem(chunk, 2)
        return pltpu.make_async_copy(
            fresh.at[slot], next_ref.at[:, pl.ds(chunk * BLK, BLK)], fresh_sem.at[slot]
        )

    def staged_copy(part):
        span = pl.ds(part * PART, PART)
        return pltpu.make_async_copy(staged.at[span], out_ref.at[span], out_sem.at[part])

    @pl.loop(0, BX)
    def _(chunk):
        for copy in load_copies(pairs, load_sem, chunk):
            copy.start()
        vel_copy(chunk).start()

    barrier = pltpu.get_barrier_semaphore()
    for near in x_near:
        pl.semaphore_signal(barrier, inc=1, device_id=(near, tile), device_id_type=MESH)
    for near in y_near:
        pl.semaphore_signal(barrier, inc=1, device_id=(stream, near), device_id_type=MESH)
    pl.semaphore_wait(barrier, 4)

    for side in range(2):
        for copy in x_copies(side):
            copy.start()

    blocks[BX * BZ] = jnp.zeros((BLK, BLK * BLK), bf16)

    @pl.loop(0, BX)
    def _(chunk):
        for copy in load_copies(pairs, load_sem, chunk):
            copy.wait()
        vel_copy(chunk).wait()

        @pl.loop(0, BLK, unroll=2)
        def _(plane):
            at = chunk * BLK + plane
            for side in range(2):
                rows = pl.ds(side * 16, 16)
                keep = slice(side * 8, side * 8 + 8)
                wet = spacer_in[at + 1, pl.ds(side * 24, 8), :] > 0
                put = pl.ds(plane * 8, 8)

                def part(ref, *index):
                    return ref[(*index, rows, slice(None))].astype(f32)[keep]

                edge_rows[side, 0, put, :] = part(conc_in, 0, at + 1)
                edge_rows[side, 1, put, :] = part(conc_in, 1, at + 1)
                edge_rows[side, 2, put, :] = jnp.where(wet, part(diff_in, at + 1), 0.0)
                edge_rows[side, 3, put, :] = part(pot_in, at + 1)
                for number in range(3):
                    edge_rows[side, 4 + number, put, :] = jnp.where(
                        wet, part(vel_in, number, at), 0.0
                    )

        for side in range(2):
            for number in range(7):
                y_send[side, number, pl.ds(chunk * BLK, BLK), :] = edge_rows[
                    side, number, pl.ds(side * 7, BLK, stride=8), :
                ].astype(bf16)
            y_copy(side, chunk).start()

    for side in range(2):
        for copy in x_copies(side):
            copy.wait_recv()

    for side, plane in ((0, 0), (1, NXL + 1)):
        wet = spacer_in[plane] > 0
        x_out[side, 3] = pot_in[plane]
        for number in range(3):
            x_out[side, number] = jnp.where(
                wet, vel_edge[side, number].astype(f32), 0.0
            ).astype(bf16)
    x_out_copy = pltpu.make_async_copy(x_out, xhalo_ref, halo_sem.at[0])
    x_out_copy.start()

    def fields_of(first, second, openness, pot):
        root = openness * lax.rsqrt(jnp.maximum(openness, 1e-20))
        level = 0.5 * pot
        flux_first = root * first
        flux_second = root * second
        return (
            flux_first + level * flux_first,
            flux_first,
            flux_second - level * flux_second,
            flux_second,
            root,
            root * level,
        )

    near = near_ref[...]

    @pl.loop(0, BX)
    def _(chunk):
        start = chunk * BLK

        @pl.loop(0, BLK + 2, unroll=2)
        def _(plane):
            at = start + plane
            openness = jnp.where(spacer_in[at] > 0, diff_in[at].astype(f32), 0.0)
            fields = fields_of(
                conc_in[0, at].astype(f32), conc_in[1, at].astype(f32), openness, pot_in[at].astype(f32)
            )
            for number, field in enumerate(fields):
                wide[number, pl.ds(plane * ROWS + LOW, NYL), :] = field
                half[number, plane] = field.astype(bf16)

        for side in range(2):
            y_copy(side, chunk).wait_recv()
        for side, row in ((0, LOW - 1), (1, LOW + NYL)):
            fields = fields_of(
                *[y_recv[side, number, pl.ds(start, BLK), :].astype(f32) for number in range(4)]
            )
            for number, field in enumerate(fields):
                wide[number, pl.ds(ROWS + row, BLK, stride=ROWS), :] = field

        @pl.when(chunk >= 2)
        def _():
            fresh_copy(chunk - 2).wait()

        slot = lax.rem(chunk, 2)

        @pl.loop(0, BLK // GROUP)
        def _(group):
            first = group * GROUP
            depth = []
            for number in range(6):
                centre = half[number, pl.ds(first + 1, GROUP)]
                sides = half[number, pl.ds(first, GROUP)] + half[number, pl.ds(first + 2, GROUP)]
                rows = jnp.concatenate([centre, sides], axis=2).reshape(GROUP * NYL, 2 * NZL)
                depth.append(jnp.dot(rows, near, preferred_element_type=f32))
            for plane in range(GROUP):
                base = (first + plane + 1) * ROWS + LOW
                total = []
                for number in range(6):
                    total.append(
                        depth[number][plane * NYL : (plane + 1) * NYL]
                        + (
                            wide[number, pl.ds(base - 1, NYL), :]
                            + wide[number, pl.ds(base + 1, NYL), :]
                        )
                    )
                at = start + first + plane + 1
                level = 0.5 * pot_in[at].astype(f32)
                root = ion_step * wide[4, pl.ds(base, NYL), :]
                tilt = level * total[4] - total[5]
                dens = conc_in[0, at].astype(f32)
                flux = total[0] - level * total[1] - dens * (total[4] + tilt)
                new_first = (dens + species_diff[0] * root * flux).astype(bf16)
                dens = conc_in[1, at].astype(f32)
                flux = total[2] + level * total[3] - dens * (total[4] - tilt)
                new_second = (dens + species_diff[1] * root * flux).astype(bf16)
                fresh[slot, 0, first + plane] = new_first
                fresh[slot, 1, first + plane] = new_second
                charge[pl.ds((first + plane) * NYL, NYL), :] = new_first.astype(
                    f32
                ) - new_second.astype(f32)

        fresh_copy(chunk).start()

        for line in range(NYL // 4):
            for part in range(4):
                lines[pl.ds(line * BLK, BLK), pl.ds(part * NZL, NZL)] = charge[
                    pl.ds(line * 4 + part, BLK, stride=NYL), :
                ].astype(bf16)
        moved = jnp.dot(lines[...], order_ref[...], preferred_element_type=f32).astype(bf16)
        for line in range(NYL // 4):
            for part in range(BZ):
                blocks[chunk * BZ + part, :, pl.ds(line * NZL, NZL)] = moved[
                    line * BLK : (line + 1) * BLK, part * NZL : (part + 1) * NZL
                ]

    y_out_copy = pltpu.make_async_copy(y_recv, yhalo_ref, halo_sem.at[1])
    y_out_copy.start()

    @pl.loop(0, slots // PART)
    def _(part):
        @pl.loop(0, PART)
        def _(number):
            staged[part * PART + number] = blocks[source_ref[part * PART + number]]

        staged_copy(part).start()

    for chunk in (BX - 2, BX - 1):
        fresh_copy(chunk).wait()
    x_out_copy.wait()
    y_out_copy.wait()
    for side in range(2):
        for copy in x_copies(side):
            copy.wait_send()

    @pl.loop(0, BX)
    def _(chunk):
        for side in range(2):
            y_copy(side, chunk).wait_send()

    @pl.loop(0, slots // PART)
    def _(part):
        staged_copy(part).wait()


def flow_kernel(
    vel_ref, pot_ref, spacer_ref, conc_ref, x_ref, y_ref, stencil_ref,
    out_ref, next_ref,
    vel_in, pot_in, spacer_in, wide, half,
    load_sem,
):
    step = pl.program_id(0)
    pairs = ((vel_ref, vel_in, 1), (pot_ref, pot_in, 0), (spacer_ref, spacer_in, 0))

    @pl.when(step == 0)
    def _():
        for chunk in range(BX):
            for copy in load_copies(pairs, load_sem, chunk):
                copy.start()
        for side, plane in ((0, 0), (1, NXL + 1)):
            for number in range(3):
                vel_in[number, plane] = x_ref[side, number]
            pot_in[plane] = x_ref[side, 3]
            spacer_in[plane] = jnp.ones((NYL, NZL), jnp.int32)

    wait_chunks(step, pairs, load_sem)
    start = step * BLK

    @pl.loop(0, BLK + 2, unroll=2)
    def _(plane):
        at = start + plane
        open_cells = spacer_in[at] > 0
        for number in range(3):
            field = jnp.where(open_cells, vel_in[number, at].astype(f32), 0.0)
            wide[number, pl.ds(plane * ROWS + LOW, NYL), :] = field
            half[number, plane] = field.astype(bf16)
        wide[3, pl.ds(plane * ROWS + LOW, NYL), :] = pot_in[at].astype(f32)

    next_ref[...] = conc_ref[...]

    for side, row in ((0, LOW - 1), (1, LOW + NYL)):
        for number, source in ((0, 4), (1, 5), (2, 6), (3, 3)):
            wide[number, pl.ds(ROWS + row, BLK, stride=ROWS), :] = y_ref[side, source].astype(f32)

    stencil = stencil_ref[...]

    @pl.loop(0, BLK // GROUP)
    def _(group):
        first = group * GROUP
        depth = []
        for number in range(3):
            rows = half[number, pl.ds(first + 1, GROUP)].reshape(GROUP * NYL, NZL)
            depth.append(jnp.dot(rows, stencil, preferred_element_type=f32))
        rows = pot_in[pl.ds(start + first + 1, GROUP)].reshape(GROUP * NYL, NZL)
        pot_depth = jnp.dot(rows, stencil[:, NZL:], preferred_element_type=f32)
        for plane in range(GROUP):
            base = (first + plane + 1) * ROWS + LOW
            span = slice(plane * NYL, (plane + 1) * NYL)
            open_cells = spacer_in[start + first + plane + 1] > 0

            def near(number, offset):
                return wide[number, pl.ds(base + offset, NYL), :]

            charge = conc_ref[0, first + plane].astype(f32) - conc_ref[1, first + plane].astype(f32)
            centre = [near(number, 0) for number in range(3)]
            slopes = (
                near(3, ROWS) - near(3, -ROWS),
                near(3, 1) - near(3, -1),
                pot_depth[span],
            )
            for number in range(3):
                front, back = near(number, ROWS), near(number, -ROWS)
                right, left = near(number, 1), near(number, -1)
                total = (front + back) + (right + left) + depth[number][span, :NZL]
                carried = (
                    centre[0] * (front - back)
                    + centre[1] * (right - left)
                    + centre[2] * depth[number][span, NZL:]
                )
                value = (1.0 - 6.0 * flow_step * viscosity) * centre[number] + (
                    flow_step * viscosity
                ) * total - (0.5 * flow_step) * (carried + charge * slopes[number])
                out_ref[number, first + plane] = jnp.where(open_cells, value, 0.0).astype(bf16)


def any_spec():
    return pl.BlockSpec(memory_space=pl.ANY)


def whole_spec(shape):
    return pl.BlockSpec(shape, lambda step: (0,) * len(shape))


def vmem_spec():
    return pl.BlockSpec(memory_space=pltpu.VMEM)


def run_ions(source, concentration, potential, diffusivity, spacer, velocity):
    near = jnp.asarray(np.concatenate([near_sum_matrix(), np.eye(NZL, dtype=np.float32)]), bf16)
    order = jnp.asarray(block_order_matrix(), bf16)
    slots = source.shape[0]
    plane = (NXL + 2, NYL, NZL)
    dma = pltpu.SemaphoreType.DMA
    return pl.pallas_call(
        ion_kernel,
        in_specs=[pl.BlockSpec(memory_space=pltpu.SMEM)] + [any_spec()] * 5 + [vmem_spec()] * 2,
        out_specs=[any_spec()] * 4,
        out_shape=[
            jax.ShapeDtypeStruct(concentration.shape, bf16),
            jax.ShapeDtypeStruct((slots, BLK, BLK * BLK), bf16),
            jax.ShapeDtypeStruct((2, 7, NXL, NZL), bf16),
            jax.ShapeDtypeStruct((2, 4, NYL, NZL), bf16),
        ],
        scratch_shapes=[
            pltpu.VMEM((2,) + plane, bf16),
            pltpu.VMEM(plane, bf16),
            pltpu.VMEM(plane, bf16),
            pltpu.VMEM(plane, jnp.int32),
            pltpu.VMEM(velocity.shape, bf16),
            pltpu.VMEM((2, 3, NYL, NZL), bf16),
            pltpu.VMEM((2, 7, BLK * 8, NZL), f32),
            pltpu.VMEM((2, 7, NXL, NZL), bf16),
            pltpu.VMEM((2, 7, NXL, NZL), bf16),
            pltpu.VMEM((2, 4, NYL, NZL), bf16),
            pltpu.VMEM((6, (BLK + 2) * ROWS, NZL), f32),
            pltpu.VMEM((6, BLK + 2, NYL, NZL), bf16),
            pltpu.VMEM((BLK * NYL, NZL), f32),
            pltpu.VMEM((NYL // 4 * BLK, 4 * NZL), bf16),
            pltpu.VMEM((BX * BZ + 1, BLK, BLK * BLK), bf16),
            pltpu.VMEM((slots, BLK, BLK * BLK), bf16),
            pltpu.VMEM((2, 2, BLK, NYL, NZL), bf16),
            dma((4, BX)),
            dma((BX,)),
            dma((2, 5)),
            dma((2, 5)),
            dma((2, BX)),
            dma((2, BX)),
            dma((2,)),
            dma((slots // PART,)),
            dma((2,)),
        ],
        compiler_params=pltpu.CompilerParams(
            vmem_limit_bytes=58 * 1024 * 1024, collective_id=0, has_side_effects=True
        ),
        cost_estimate=pl.CostEstimate(flops=200_000_000, bytes_accessed=17_000_000, transcendentals=0),
        name="ions",
    )(source, concentration, potential, diffusivity, spacer, velocity, near, order)


def run_flow(velocity, potential, spacer, conc_next, xhalo, yhalo):
    stencil = jnp.asarray(np.concatenate([near_sum_matrix(), difference_matrix()], axis=1), bf16)
    plane = (NXL + 2, NYL, NZL)
    return pl.pallas_call(
        flow_kernel,
        grid=(BX,),
        in_specs=[
            any_spec(), any_spec(), any_spec(),
            pl.BlockSpec((2, BLK, NYL, NZL), lambda step: (0, step, 0, 0)),
            whole_spec(xhalo.shape),
            pl.BlockSpec((2, 7, BLK, NZL), lambda step: (0, 0, step, 0)),
            whole_spec(stencil.shape),
        ],
        out_specs=[
            pl.BlockSpec((3, BLK, NYL, NZL), lambda step: (0, step, 0, 0)),
            pl.BlockSpec((2, BLK, NYL, NZL), lambda step: (0, step, 0, 0)),
        ],
        out_shape=[
            jax.ShapeDtypeStruct(velocity.shape, bf16),
            jax.ShapeDtypeStruct(conc_next.shape, bf16),
        ],
        scratch_shapes=[
            pltpu.VMEM((3,) + plane, bf16),
            pltpu.VMEM(plane, bf16),
            pltpu.VMEM(plane, jnp.int32),
            pltpu.VMEM((4, (BLK + 2) * ROWS, NZL), f32),
            pltpu.VMEM((3, BLK + 2, NYL, NZL), bf16),
            pltpu.SemaphoreType.DMA((3, BX)),
        ],
        compiler_params=pltpu.CompilerParams(vmem_limit_bytes=58 * 1024 * 1024),
        cost_estimate=pl.CostEstimate(flops=200_000_000, bytes_accessed=17_000_000, transcendentals=0),
        name="flow",
    )(velocity, potential, spacer, conc_next, xhalo, yhalo, stencil)


def per_device(concentration, potential, diffusivity, spacer, velocity, balance_plan):
    tiles = lax.axis_size("tile")
    count = balance_plan.shape[0]
    capacity = max(2, (2 * count + tiles - 1) // tiles)
    slots = tiles * capacity

    owners = balance_plan[:, 0]
    number = jnp.arange(count, dtype=jnp.int32)
    same_owner = owners[:, None] == owners[None, :]
    earlier = number[:, None] < number[None, :]
    ranking = jnp.sum(jnp.logical_and(same_owner, earlier).astype(jnp.int32), axis=0)
    target = owners * capacity + ranking
    named = target[None, :] == jnp.arange(slots, dtype=jnp.int32)[:, None]
    source = count + jnp.sum(jnp.where(named, number[None, :] - count, 0), axis=1)

    conc_next, outgoing, yhalo, xhalo = run_ions(
        source, concentration, potential, diffusivity, spacer, velocity
    )
    outgoing = outgoing.reshape(tiles, capacity, BLK, BLK * BLK)
    owned = lax.all_to_all(outgoing, "tile", split_axis=0, concat_axis=0, tiled=True)
    owned = owned.reshape(slots, BLK, BLK * BLK)

    flow_next, conc_next = run_flow(velocity, potential, spacer, conc_next, xhalo, yhalo)
    return (conc_next, flow_next, owned)


def solution(mesh):
    placed = (
        P(None, "stream", "tile", None),
        P("stream", "tile", None),
        P("stream", "tile", None),
        P("stream", "tile", None),
        P(None, "stream", "tile", None),
        P(("stream", "tile"), None),
    )
    return jax.shard_map(
        per_device,
        mesh=mesh,
        in_specs=placed,
        out_specs=(
            P(None, "stream", "tile", None),
            P(None, "stream", "tile", None),
            P(("stream", "tile"), None, None),
        ),
        check_vma=False,
    )
```

time: 130 us -> 99.1 us (0.76)
  waiting for transfers between devices: 49.3 us -> 36.1 us
  starting transfers between devices: 18.6 us -> 9.47 us
  local copies, waits for them, and re-layouts: 13.9 us -> 5.01 us
    ppermute x8 -> x0, waiting for transfers between devices: 49.3 us -> none  [the longest x4 44.7 us: exchange(): lax.ppermute(high_edge, axis, forward)]
    all_to_all x1, waiting for transfers between devices: 0.01 us -> 36.1 us  [per_device(): lax.all_to_all(outgoing, 'tile', split_axis=0, concat_axis=0, tiled=True)]
    ppermute x8 -> x0, starting transfers between devices: 10.3 us -> none  [the longest x4 7.25 us: exchange(): lax.ppermute(high_edge, axis, forward)]
    slice x9 -> x0, local copies, waits for them, and re-layouts: 7.9 us -> none  [the longest x5 7.88 us: cut(): return lax.index_in_dim(array, index, dim, keepdims=False)]
    select_n x5 -> x0, other arithmetic: 2.03 us -> none  [the longest x2 1.06 us: edges_of(): openness = jnp.where(solid, cut(diffusivity, dim, index), 0)[None]]
    unnamed x19 -> x1, local copies, waits for them, and re-layouts: 5.1 us -> 5.01 us
  transfers between devices with their start and end apart: 9 -> 1, of which waited for: 4 -> 1; matrix products, arithmetic and copies ran while one was open for 7% -> 0% of each run, Pallas kernels for 13% -> 17%
where the time goes in v2:
time: 99.1 us; the launch traced here: 97.8 us
  Pallas kernels  44.6 us (45%)
  waiting for transfers between devices  36.1 us (36%)
  starting transfers between devices  9.47 us (10%)
  local copies, waits for them, and re-layouts  5.01 us (5%)
  other arithmetic  2.09 us (2%)
    all_to_all x1, waiting for transfers between devices, per_device(): lax.all_to_all(outgoing, 'tile', split_axis=0, concat_axis=0, tiled=True)  36.1 us
    pallas_call x1, Pallas kernels, run_ions(): pl.pallas_call(ion_kernel, in_specs=[pl.BlockSpec(memory_space=pltpu.SMEM...  28.3 us
    pallas_call x1, Pallas kernels, run_flow(): pl.pallas_call(flow_kernel, grid=(BX,), in_specs=[any_spec(), any_spec(),...  16.2 us
    all_to_all x1, starting transfers between devices, per_device(): lax.all_to_all(outgoing, 'tile', split_axis=0, concat_axis=0, tiled=True)  9.47 us
    unnamed x1, local copies, waits for them, and re-layouts  5.01 us
  transfers between devices with their start and end apart: 1, of which 1 were waited for; matrix products, arithmetic and copies ran while one was open for 0% of the time, Pallas kernels for 17%

profile of v2, /device:TPU:1, one launch (start us, length us, event | category | flops | bytes accessed | tf_op | source)
XLA Modules:
  0.0 97.8 jit_solution(1388177502559439987)
XLA Ops:
  0.6 0.8 convert_reduce_fusion
  1.4 0.7 iota_add_fusion
  2.1 0.1 select_reduce_fusion
  2.2 0.5 broadcast_add_fusion.source_ref
  2.7 28.3 %ions.1 = (bf16[2,192,32,128]{3,2,1,0:T(8,128)(2,1)}, bf16[64,32,1024]{2,1,0:T(8,128)(2,1)}, bf16[2,7,192,128]{3,2,1,0:T(8,128)(2,1)}, bf16[2,4,32,128]{3,2,1,0:T(8,128)(2,1)}) custom-call(s32[64]{0:T(128)} %broadcast_add_fusion.source_ref, bf16[2,192,32,128]{3,2,1,0:T(8,128)(2,1)} %conc_ref.1, bf16[192,32,128]{2,1,0:T(8,128)(2,1)} %pot_ref.3, ...), custom_call_target="tpu_custom_call" | custom-call | flops 200000000 | bytes 17000000 | tf_op jit(solution)/shard_map/ions/pallas_call | solution.py:432
  31.1 9.5 %all-to-all-start = ((bf16[32,2,32,1024]{3,2,1,0:T(8,128)(2,1)}), bf16[32,2,32,1024]{3,2,1,0:T(8,128)(2,1)}, u32[]{:S(2)}, u32[]{:S(2)}) async-start(bf16[32,2,32,1024]{3,2,1,0:T(8,128)(2,1)} %bitcast.4), calls=%async_computation | async-start | bytes 8388608 | tf_op jit(solution)/shard_map/all_to_all | solution.py:532
  40.5 16.2 %flow.1 = (bf16[3,192,32,128]{3,2,1,0:T(8,128)(2,1)}, bf16[2,192,32,128]{3,2,1,0:T(8,128)(2,1)}) custom-call(bf16[3,192,32,128]{3,2,1,0:T(8,128)(2,1)} %vel_ref.3, bf16[192,32,128]{2,1,0:T(8,128)(2,1)} %pot_ref.3, s32[192,32,128]{2,1,0:T(8,128)} %spacer_ref.3, bf16[2,192,32,128]{3,2,1,0:T(8,128)(2,1)} %get-tuple-element.9.conc_ref, ...), custom_call_target="tpu_custom_call" | custom-call | flops 200000000 | bytes 17000000 | tf_op jit(solution)/shard_map/flow/pallas_call | solution.py:481
  56.8 36.1 %all-to-all-done = bf16[32,2,32,1024]{3,2,1,0:T(8,128)(2,1)} async-done(((bf16[32,2,32,1024]{3,2,1,0:T(8,128)(2,1)}), bf16[32,2,32,1024]{3,2,1,0:T(8,128)(2,1)}, u32[]{:S(2)}, u32[]{:S(2)}) %all-to-all-start) | async-done | bytes 4194336 | tf_op jit(solution)/shard_map/all_to_all | solution.py:532
  92.8 5.0 %copy.13 = bf16[64,32,1024]{2,1,0:T(8,128)(2,1)} copy(bf16[64,32,1024]{2,1,0:T(8,128)(2,1)} %bitcast.2) | data formatting | bytes 8388608
Async XLA Ops:
  31.1 61.8 %all-to-all-start = ((bf16[32,2,32,1024]{3,2,1,0:T(8,128)(2,1)}), bf16[32,2,32,1024]{3,2,1,0:T(8,128)(2,1)}, u32[]{:S(2)}, u32[]{:S(2)}) async-start(bf16[32,2,32,1024]{3,2,1,0:T(8,128)(2,1)} %bitcast.4), calls=%async_computation | async-start | bytes 8388608 | tf_op jit(solution)/shard_map/all_to_all | solution.py:532

commit v3 on v2

--- a/solution.py
+++ b/solution.py
@@ -14,8 +14,9 @@
 NZL = BZ * BLK
 ROWS = 48
 LOW = 8
-GROUP = 8
+GROUP = 32
 PART = 8
+COPIES = 16
 
 MESH = pl.DeviceIdType.MESH
 
@@ -74,10 +75,10 @@
 
 
 def ion_kernel(
-    source_ref, conc_ref, pot_ref, diff_ref, spacer_ref, vel_ref, near_ref, order_ref,
+    plan_ref, conc_ref, pot_ref, diff_ref, spacer_ref, vel_ref, near_ref, order_ref,
     next_ref, out_ref, yhalo_ref, xhalo_ref,
     conc_in, pot_in, diff_in, spacer_in, vel_in, vel_edge, edge_rows, y_send, y_recv, x_out,
-    wide, half, charge, lines, blocks, staged, fresh,
+    wide, half, charge, lines, blocks, staged, fresh, source_ref,
     load_sem, vel_sem, xs_sem, xr_sem, ys_sem, yr_sem, fresh_sem, out_sem, halo_sem,
 ):
     slots = out_ref.shape[0]
@@ -150,6 +151,17 @@
         pl.semaphore_signal(barrier, inc=1, device_id=(near, tile), device_id_type=MESH)
     for near in y_near:
         pl.semaphore_signal(barrier, inc=1, device_id=(stream, near), device_id_type=MESH)
+
+    @pl.loop(0, tiles)
+    def _(owner):
+        first = second = jnp.int32(BX * BZ)
+        for block in reversed(range(BX * BZ)):
+            named = plan_ref[block] == owner
+            second = jnp.where(named, first, second)
+            first = jnp.where(named, block, first)
+        source_ref[2 * owner] = first
+        source_ref[2 * owner + 1] = second
+
     pl.semaphore_wait(barrier, 4)
 
     for side in range(2):
@@ -164,7 +176,7 @@
             copy.wait()
         vel_copy(chunk).wait()
 
-        @pl.loop(0, BLK, unroll=2)
+        @pl.loop(0, BLK, unroll=8)
         def _(plane):
             at = chunk * BLK + plane
             for side in range(2):
@@ -226,7 +238,7 @@
     def _(chunk):
         start = chunk * BLK
 
-        @pl.loop(0, BLK + 2, unroll=2)
+        @pl.loop(0, BLK + 2, unroll=17)
         def _(plane):
             at = start + plane
             openness = jnp.where(spacer_in[at] > 0, diff_in[at].astype(f32), 0.0)
@@ -354,7 +366,7 @@
     wait_chunks(step, pairs, load_sem)
     start = step * BLK
 
-    @pl.loop(0, BLK + 2, unroll=2)
+    @pl.loop(0, BLK + 2, unroll=17)
     def _(plane):
         at = start + plane
         open_cells = spacer_in[at] > 0
@@ -423,10 +435,9 @@
     return pl.BlockSpec(memory_space=pltpu.VMEM)
 
 
-def run_ions(source, concentration, potential, diffusivity, spacer, velocity):
+def run_ions(plan, slots, concentration, potential, diffusivity, spacer, velocity):
     near = jnp.asarray(np.concatenate([near_sum_matrix(), np.eye(NZL, dtype=np.float32)]), bf16)
     order = jnp.asarray(block_order_matrix(), bf16)
-    slots = source.shape[0]
     plane = (NXL + 2, NYL, NZL)
     dma = pltpu.SemaphoreType.DMA
     return pl.pallas_call(
@@ -457,6 +468,7 @@
             pltpu.VMEM((BX * BZ + 1, BLK, BLK * BLK), bf16),
             pltpu.VMEM((slots, BLK, BLK * BLK), bf16),
             pltpu.VMEM((2, 2, BLK, NYL, NZL), bf16),
+            pltpu.SMEM((slots,), jnp.int32),
             dma((4, BX)),
             dma((BX,)),
             dma((2, 5)),
@@ -472,7 +484,40 @@
         ),
         cost_estimate=pl.CostEstimate(flops=200_000_000, bytes_accessed=17_000_000, transcendentals=0),
         name="ions",
-    )(source, concentration, potential, diffusivity, spacer, velocity, near, order)
+    )(plan, concentration, potential, diffusivity, spacer, velocity, near, order)
+
+
+def owned_kernel(part_ref, out_ref, held, in_sem, out_sem):
+    size = held.shape[0] // COPIES
+
+    def copy(number, source, target, sem):
+        rows = pl.ds(number * size, size)
+        return pltpu.make_async_copy(source.at[rows], target.at[rows], sem.at[number])
+
+    for number in range(COPIES):
+        copy(number, part_ref, held, in_sem).start()
+    for number in range(COPIES):
+        copy(number, part_ref, held, in_sem).wait()
+        copy(number, held, out_ref, out_sem).start()
+    for number in range(COPIES):
+        copy(number, held, out_ref, out_sem).wait()
+
+
+def put_owned(part):
+    return pl.pallas_call(
+        owned_kernel,
+        in_specs=[any_spec()],
+        out_specs=any_spec(),
+        out_shape=jax.ShapeDtypeStruct(part.shape, bf16),
+        scratch_shapes=[
+            pltpu.VMEM(part.shape, bf16),
+            pltpu.SemaphoreType.DMA((COPIES,)),
+            pltpu.SemaphoreType.DMA((COPIES,)),
+        ],
+        compiler_params=pltpu.CompilerParams(vmem_limit_bytes=58 * 1024 * 1024),
+        cost_estimate=pl.CostEstimate(flops=0, bytes_accessed=8_400_000, transcendentals=0),
+        name="owned",
+    )(part)
 
 
 def run_flow(velocity, potential, spacer, conc_next, xhalo, yhalo):
@@ -512,25 +557,14 @@
 
 def per_device(concentration, potential, diffusivity, spacer, velocity, balance_plan):
     tiles = lax.axis_size("tile")
-    count = balance_plan.shape[0]
-    capacity = max(2, (2 * count + tiles - 1) // tiles)
+    capacity = 2
     slots = tiles * capacity
-
-    owners = balance_plan[:, 0]
-    number = jnp.arange(count, dtype=jnp.int32)
-    same_owner = owners[:, None] == owners[None, :]
-    earlier = number[:, None] < number[None, :]
-    ranking = jnp.sum(jnp.logical_and(same_owner, earlier).astype(jnp.int32), axis=0)
-    target = owners * capacity + ranking
-    named = target[None, :] == jnp.arange(slots, dtype=jnp.int32)[:, None]
-    source = count + jnp.sum(jnp.where(named, number[None, :] - count, 0), axis=1)
-
     conc_next, outgoing, yhalo, xhalo = run_ions(
-        source, concentration, potential, diffusivity, spacer, velocity
+        balance_plan[:, 0], slots, concentration, potential, diffusivity, spacer, velocity
     )
     outgoing = outgoing.reshape(tiles, capacity, BLK, BLK * BLK)
     owned = lax.all_to_all(outgoing, "tile", split_axis=0, concat_axis=0, tiled=True)
-    owned = owned.reshape(slots, BLK, BLK * BLK)
+    owned = put_owned(owned.reshape(slots, BLK, BLK * BLK))
 
     flow_next, conc_next = run_flow(velocity, potential, spacer, conc_next, xhalo, yhalo)
     return (conc_next, flow_next, owned)

time: 99.1 us -> 93 us (0.938)
  local copies, waits for them, and re-layouts: 5.01 us -> 0 us
  waiting for transfers between devices: 36.1 us -> 38.5 us
  other arithmetic: 2.09 us -> 0 us
  Pallas kernels: 44.6 us -> 43.2 us
    unnamed x1 -> x0, local copies, waits for them, and re-layouts: 5.01 us -> none
    pallas_call x0 -> x1, Pallas kernels: none -> 3.85 us  [put_owned(): pl.pallas_call(owned_kernel, in_specs=[any_spec()], out_specs=any_spec(),...]
    pallas_call x1, Pallas kernels: 28.3 us -> 25.6 us  [run_ions(): pl.pallas_call(ion_kernel, in_specs=[pl.BlockSpec(memory_space=pltpu.SMEM...]
    pallas_call x1, Pallas kernels: 16.2 us -> 13.8 us  [run_flow(): pl.pallas_call(flow_kernel, grid=(BX,), in_specs=[any_spec(), any_spec(),...]
    all_to_all x1, waiting for transfers between devices: 36.1 us -> 38.5 us  [per_device(): lax.all_to_all(outgoing, 'tile', split_axis=0, concat_axis=0, tiled=True)]
  transfers between devices with their start and end apart: 1 -> 1, of which waited for: 1 -> 1; matrix products, arithmetic and copies ran while one was open for 0% -> 0% of each run, Pallas kernels for 17% -> 15%
where the time goes in v3:
time: 93 us; the launch traced here: 91.8 us
  Pallas kernels  43.2 us (46%)
  waiting for transfers between devices  38.5 us (41%)
  starting transfers between devices  9.43 us (10%)
    all_to_all x1, waiting for transfers between devices, per_device(): lax.all_to_all(outgoing, 'tile', split_axis=0, concat_axis=0, tiled=True)  38.5 us
    pallas_call x1, Pallas kernels, run_ions(): pl.pallas_call(ion_kernel, in_specs=[pl.BlockSpec(memory_space=pltpu.SMEM...  25.6 us
    pallas_call x1, Pallas kernels, run_flow(): pl.pallas_call(flow_kernel, grid=(BX,), in_specs=[any_spec(), any_spec(),...  13.8 us
    all_to_all x1, starting transfers between devices, per_device(): lax.all_to_all(outgoing, 'tile', split_axis=0, concat_axis=0, tiled=True)  9.43 us
    pallas_call x1, Pallas kernels, put_owned(): pl.pallas_call(owned_kernel, in_specs=[any_spec()], out_specs=any_spec(),...  3.85 us
  transfers between devices with their start and end apart: 1, of which 1 were waited for; matrix products, arithmetic and copies ran while one was open for 0% of the time, Pallas kernels for 15%

profile of v3, /device:TPU:1, one launch (start us, length us, event | category | flops | bytes accessed | tf_op | source)
XLA Modules:
  0.0 91.8 jit_solution(460432435630888435)
XLA Ops:
  0.6 25.6 %ions.1 = (bf16[2,192,32,128]{3,2,1,0:T(8,128)(2,1)}, bf16[64,32,1024]{2,1,0:T(8,128)(2,1)}, bf16[2,7,192,128]{3,2,1,0:T(8,128)(2,1)}, bf16[2,4,32,128]{3,2,1,0:T(8,128)(2,1)}) custom-call(s32[24]{0:T(128)} %bitcast.4, bf16[2,192,32,128]{3,2,1,0:T(8,128)(2,1)} %conc_ref.1, bf16[192,32,128]{2,1,0:T(8,128)(2,1)} %pot_ref.3, bf16[192,32,128]{2,1,0:T(8,128)(2,1)} %diff_ref.1, ...), custom_call_target="tpu_custom_call" | custom-call | flops 200000000 | bytes 17000000 | tf_op jit(solution)/shard_map/ions/pallas_call | solution.py:443
  26.2 9.4 %all-to-all-start = ((bf16[32,2,32,1024]{3,2,1,0:T(8,128)(2,1)}), bf16[32,2,32,1024]{3,2,1,0:T(8,128)(2,1)}, u32[]{:S(2)}, u32[]{:S(2)}) async-start(bf16[32,2,32,1024]{3,2,1,0:T(8,128)(2,1)} %bitcast.3), calls=%async_computation | async-start | bytes 8388608 | tf_op jit(solution)/shard_map/all_to_all | solution.py:566
  35.6 13.8 %flow.1 = (bf16[3,192,32,128]{3,2,1,0:T(8,128)(2,1)}, bf16[2,192,32,128]{3,2,1,0:T(8,128)(2,1)}) custom-call(bf16[3,192,32,128]{3,2,1,0:T(8,128)(2,1)} %vel_ref.3, bf16[192,32,128]{2,1,0:T(8,128)(2,1)} %pot_ref.3, s32[192,32,128]{2,1,0:T(8,128)} %spacer_ref.3, bf16[2,192,32,128]{3,2,1,0:T(8,128)(2,1)} %get-tuple-element.9.conc_ref, ...), custom_call_target="tpu_custom_call" | custom-call | flops 200000000 | bytes 17000000 | tf_op jit(solution)/shard_map/flow/pallas_call | solution.py:526
  49.4 38.5 %all-to-all-done = bf16[32,2,32,1024]{3,2,1,0:T(8,128)(2,1)} async-done(((bf16[32,2,32,1024]{3,2,1,0:T(8,128)(2,1)}), bf16[32,2,32,1024]{3,2,1,0:T(8,128)(2,1)}, u32[]{:S(2)}, u32[]{:S(2)}) %all-to-all-start) | async-done | bytes 4194336 | tf_op jit(solution)/shard_map/all_to_all | solution.py:566
  87.9 3.8 %owned.1 = bf16[64,32,1024]{2,1,0:T(8,128)(2,1)} custom-call(bf16[64,32,1024]{2,1,0:T(8,128)(2,1)} %bitcast.2.part_ref), custom_call_target="tpu_custom_call" | custom-call | bytes 8400000 | tf_op jit(solution)/shard_map/owned/pallas_call | solution.py:507
Async XLA Ops:
  26.2 61.7 %all-to-all-start = ((bf16[32,2,32,1024]{3,2,1,0:T(8,128)(2,1)}), bf16[32,2,32,1024]{3,2,1,0:T(8,128)(2,1)}, u32[]{:S(2)}, u32[]{:S(2)}) async-start(bf16[32,2,32,1024]{3,2,1,0:T(8,128)(2,1)} %bitcast.3), calls=%async_computation | async-start | bytes 8388608 | tf_op jit(solution)/shard_map/all_to_all | solution.py:566

commit v4 on v3

--- a/solution.py
+++ b/solution.py
@@ -119,13 +119,14 @@
             for number, (source, target) in enumerate(ends)
         ]
 
-    def y_copy(side, chunk):
+    def y_copy(side, chunk, kind):
         span = pl.ds(chunk * BLK, BLK)
+        fields = (pl.ds(0, 4), pl.ds(4, 3))[kind]
         return pltpu.make_async_remote_copy(
-            src_ref=y_send.at[side, :, span],
-            dst_ref=y_recv.at[1 - side, :, span],
-            send_sem=ys_sem.at[side, chunk],
-            recv_sem=yr_sem.at[side, chunk],
+            src_ref=y_send.at[side, fields, span],
+            dst_ref=y_recv.at[1 - side, fields, span],
+            send_sem=ys_sem.at[kind, side, chunk],
+            recv_sem=yr_sem.at[kind, side, chunk],
             device_id=(stream, y_near[side]),
             device_id_type=MESH,
         )
@@ -144,6 +145,9 @@
     def _(chunk):
         for copy in load_copies(pairs, load_sem, chunk):
             copy.start()
+
+    @pl.loop(0, BX)
+    def _(chunk):
         vel_copy(chunk).start()
 
     barrier = pltpu.get_barrier_semaphore()
@@ -170,12 +174,7 @@
 
     blocks[BX * BZ] = jnp.zeros((BLK, BLK * BLK), bf16)
 
-    @pl.loop(0, BX)
-    def _(chunk):
-        for copy in load_copies(pairs, load_sem, chunk):
-            copy.wait()
-        vel_copy(chunk).wait()
-
+    def pack_edges(chunk, kind):
         @pl.loop(0, BLK, unroll=8)
         def _(plane):
             at = chunk * BLK + plane
@@ -188,21 +187,29 @@
                 def part(ref, *index):
                     return ref[(*index, rows, slice(None))].astype(f32)[keep]
 
-                edge_rows[side, 0, put, :] = part(conc_in, 0, at + 1)
-                edge_rows[side, 1, put, :] = part(conc_in, 1, at + 1)
-                edge_rows[side, 2, put, :] = jnp.where(wet, part(diff_in, at + 1), 0.0)
-                edge_rows[side, 3, put, :] = part(pot_in, at + 1)
-                for number in range(3):
-                    edge_rows[side, 4 + number, put, :] = jnp.where(
-                        wet, part(vel_in, number, at), 0.0
-                    )
+                if kind == 0:
+                    edge_rows[side, 0, put, :] = part(conc_in, 0, at + 1)
+                    edge_rows[side, 1, put, :] = part(conc_in, 1, at + 1)
+                    edge_rows[side, 2, put, :] = jnp.where(wet, part(diff_in, at + 1), 0.0)
+                    edge_rows[side, 3, put, :] = part(pot_in, at + 1)
+                else:
+                    for number in range(3):
+                        edge_rows[side, 4 + number, put, :] = jnp.where(
+                            wet, part(vel_in, number, at), 0.0
+                        )
 
         for side in range(2):
-            for number in range(7):
+            for number in (range(4), range(4, 7))[kind]:
                 y_send[side, number, pl.ds(chunk * BLK, BLK), :] = edge_rows[
                     side, number, pl.ds(side * 7, BLK, stride=8), :
                 ].astype(bf16)
-            y_copy(side, chunk).start()
+            y_copy(side, chunk, kind).start()
+
+    @pl.loop(0, BX)
+    def _(chunk):
+        for copy in load_copies(pairs, load_sem, chunk):
+            copy.wait()
+        pack_edges(chunk, 0)
 
     for side in range(2):
         for copy in x_copies(side):
@@ -237,6 +244,8 @@
     @pl.loop(0, BX)
     def _(chunk):
         start = chunk * BLK
+        vel_copy(chunk).wait()
+        pack_edges(chunk, 1)
 
         @pl.loop(0, BLK + 2, unroll=17)
         def _(plane):
@@ -250,7 +259,7 @@
                 half[number, plane] = field.astype(bf16)
 
         for side in range(2):
-            y_copy(side, chunk).wait_recv()
+            y_copy(side, chunk, 0).wait_recv()
         for side, row in ((0, LOW - 1), (1, LOW + NYL)):
             fields = fields_of(
                 *[y_recv[side, number, pl.ds(start, BLK), :].astype(f32) for number in range(4)]
@@ -314,6 +323,11 @@
                     line * BLK : (line + 1) * BLK, part * NZL : (part + 1) * NZL
                 ]
 
+    @pl.loop(0, BX)
+    def _(chunk):
+        for side in range(2):
+            y_copy(side, chunk, 1).wait_recv()
+
     y_out_copy = pltpu.make_async_copy(y_recv, yhalo_ref, halo_sem.at[1])
     y_out_copy.start()
 
@@ -336,7 +350,8 @@
     @pl.loop(0, BX)
     def _(chunk):
         for side in range(2):
-            y_copy(side, chunk).wait_send()
+            for kind in range(2):
+                y_copy(side, chunk, kind).wait_send()
 
     @pl.loop(0, slots // PART)
     def _(part):
@@ -473,8 +488,8 @@
             dma((BX,)),
             dma((2, 5)),
             dma((2, 5)),
-            dma((2, BX)),
-            dma((2, BX)),
+            dma((2, 2, BX)),
+            dma((2, 2, BX)),
             dma((2,)),
             dma((slots // PART,)),
             dma((2,)),

time: 93 us -> 95.2 us (1.024)
  Pallas kernels: 43.2 us -> 47.6 us
  starting transfers between devices: 9.43 us -> 7.37 us
    pallas_call x1, Pallas kernels: 25.6 us -> 30 us  [run_ions(): pl.pallas_call(ion_kernel, in_specs=[pl.BlockSpec(memory_space=pltpu.SMEM...]
    all_to_all x1, starting transfers between devices: 9.43 us -> 7.37 us  [per_device(): lax.all_to_all(outgoing, 'tile', split_axis=0, concat_axis=0, tiled=True)]
where the time goes in v4:
time: 95.2 us; the launch traced here: 94.1 us
  Pallas kernels  47.6 us (50%)
  waiting for transfers between devices  38.5 us (40%)
  starting transfers between devices  7.37 us (8%)
    all_to_all x1, waiting for transfers between devices, per_device(): lax.all_to_all(outgoing, 'tile', split_axis=0, concat_axis=0, tiled=True)  38.5 us
    pallas_call x1, Pallas kernels, run_ions(): pl.pallas_call(ion_kernel, in_specs=[pl.BlockSpec(memory_space=pltpu.SMEM...  30 us
    pallas_call x1, Pallas kernels, run_flow(): pl.pallas_call(flow_kernel, grid=(BX,), in_specs=[any_spec(), any_spec(),...  13.8 us
    all_to_all x1, starting transfers between devices, per_device(): lax.all_to_all(outgoing, 'tile', split_axis=0, concat_axis=0, tiled=True)  7.37 us
    pallas_call x1, Pallas kernels, put_owned(): pl.pallas_call(owned_kernel, in_specs=[any_spec()], out_specs=any_spec(),...  3.85 us
  transfers between devices with their start and end apart: 1, of which 1 were waited for; matrix products, arithmetic and copies ran while one was open for 0% of the time, Pallas kernels for 15%

profile of v4, /device:TPU:1, one launch (start us, length us, event | category | flops | bytes accessed | tf_op | source)
XLA Modules:
  0.0 94.1 jit_solution(16134306631039815727)
XLA Ops:
  0.6 30.0 %ions.1 = (bf16[2,192,32,128]{3,2,1,0:T(8,128)(2,1)}, bf16[64,32,1024]{2,1,0:T(8,128)(2,1)}, bf16[2,7,192,128]{3,2,1,0:T(8,128)(2,1)}, bf16[2,4,32,128]{3,2,1,0:T(8,128)(2,1)}) custom-call(s32[24]{0:T(128)} %bitcast.4, bf16[2,192,32,128]{3,2,1,0:T(8,128)(2,1)} %conc_ref.1, bf16[192,32,128]{2,1,0:T(8,128)(2,1)} %pot_ref.3, bf16[192,32,128]{2,1,0:T(8,128)(2,1)} %diff_ref.1, ...), custom_call_target="tpu_custom_call" | custom-call | flops 200000000 | bytes 17000000 | tf_op jit(solution)/shard_map/ions/pallas_call | solution.py:458
  30.6 7.4 %all-to-all-start = ((bf16[32,2,32,1024]{3,2,1,0:T(8,128)(2,1)}), bf16[32,2,32,1024]{3,2,1,0:T(8,128)(2,1)}, u32[]{:S(2)}, u32[]{:S(2)}) async-start(bf16[32,2,32,1024]{3,2,1,0:T(8,128)(2,1)} %bitcast.3), calls=%async_computation | async-start | bytes 8388608 | tf_op jit(solution)/shard_map/all_to_all | solution.py:581
  38.0 13.8 %flow.1 = (bf16[3,192,32,128]{3,2,1,0:T(8,128)(2,1)}, bf16[2,192,32,128]{3,2,1,0:T(8,128)(2,1)}) custom-call(bf16[3,192,32,128]{3,2,1,0:T(8,128)(2,1)} %vel_ref.3, bf16[192,32,128]{2,1,0:T(8,128)(2,1)} %pot_ref.3, s32[192,32,128]{2,1,0:T(8,128)} %spacer_ref.3, bf16[2,192,32,128]{3,2,1,0:T(8,128)(2,1)} %get-tuple-element.9.conc_ref, ...), custom_call_target="tpu_custom_call" | custom-call | flops 200000000 | bytes 17000000 | tf_op jit(solution)/shard_map/flow/pallas_call | solution.py:541
  51.7 38.5 %all-to-all-done = bf16[32,2,32,1024]{3,2,1,0:T(8,128)(2,1)} async-done(((bf16[32,2,32,1024]{3,2,1,0:T(8,128)(2,1)}), bf16[32,2,32,1024]{3,2,1,0:T(8,128)(2,1)}, u32[]{:S(2)}, u32[]{:S(2)}) %all-to-all-start) | async-done | bytes 4194336 | tf_op jit(solution)/shard_map/all_to_all | solution.py:581
  90.2 3.8 %owned.1 = bf16[64,32,1024]{2,1,0:T(8,128)(2,1)} custom-call(bf16[64,32,1024]{2,1,0:T(8,128)(2,1)} %bitcast.2.part_ref), custom_call_target="tpu_custom_call" | custom-call | bytes 8400000 | tf_op jit(solution)/shard_map/owned/pallas_call | solution.py:522
Async XLA Ops:
  30.6 59.6 %all-to-all-start = ((bf16[32,2,32,1024]{3,2,1,0:T(8,128)(2,1)}), bf16[32,2,32,1024]{3,2,1,0:T(8,128)(2,1)}, u32[]{:S(2)}, u32[]{:S(2)}) async-start(bf16[32,2,32,1024]{3,2,1,0:T(8,128)(2,1)} %bitcast.3), calls=%async_computation | async-start | bytes 8388608 | tf_op jit(solution)/shard_map/all_to_all | solution.py:581

commit v5 on v3

--- a/solution.py
+++ b/solution.py
@@ -17,6 +17,8 @@
 GROUP = 32
 PART = 8
 COPIES = 16
+PITCH = NYL + 1
+EDGE_PITCH = 9
 
 MESH = pl.DeviceIdType.MESH
 
@@ -183,7 +185,7 @@
                 rows = pl.ds(side * 16, 16)
                 keep = slice(side * 8, side * 8 + 8)
                 wet = spacer_in[at + 1, pl.ds(side * 24, 8), :] > 0
-                put = pl.ds(plane * 8, 8)
+                put = pl.ds(plane * EDGE_PITCH, 8)
 
                 def part(ref, *index):
                     return ref[(*index, rows, slice(None))].astype(f32)[keep]
@@ -200,7 +202,7 @@
         for side in range(2):
             for number in range(7):
                 y_send[side, number, pl.ds(chunk * BLK, BLK), :] = edge_rows[
-                    side, number, pl.ds(side * 7, BLK, stride=8), :
+                    side, number, pl.ds(side * 7, BLK, stride=EDGE_PITCH), :
                 ].astype(bf16)
             y_copy(side, chunk).start()
 
@@ -296,7 +298,7 @@
                 new_second = (dens + species_diff[1] * root * flux).astype(bf16)
                 fresh[slot, 0, first + plane] = new_first
                 fresh[slot, 1, first + plane] = new_second
-                charge[pl.ds((first + plane) * NYL, NYL), :] = new_first.astype(
+                charge[pl.ds((first + plane) * PITCH, NYL), :] = new_first.astype(
                     f32
                 ) - new_second.astype(f32)
 
@@ -305,7 +307,7 @@
         for line in range(NYL // 4):
             for part in range(4):
                 lines[pl.ds(line * BLK, BLK), pl.ds(part * NZL, NZL)] = charge[
-                    pl.ds(line * 4 + part, BLK, stride=NYL), :
+                    pl.ds(line * 4 + part, BLK, stride=PITCH), :
                 ].astype(bf16)
         moved = jnp.dot(lines[...], order_ref[...], preferred_element_type=f32).astype(bf16)
         for line in range(NYL // 4):
@@ -457,13 +459,13 @@
             pltpu.VMEM(plane, jnp.int32),
             pltpu.VMEM(velocity.shape, bf16),
             pltpu.VMEM((2, 3, NYL, NZL), bf16),
-            pltpu.VMEM((2, 7, BLK * 8, NZL), f32),
+            pltpu.VMEM((2, 7, BLK * EDGE_PITCH, NZL), f32),
             pltpu.VMEM((2, 7, NXL, NZL), bf16),
             pltpu.VMEM((2, 7, NXL, NZL), bf16),
             pltpu.VMEM((2, 4, NYL, NZL), bf16),
             pltpu.VMEM((6, (BLK + 2) * ROWS, NZL), f32),
             pltpu.VMEM((6, BLK + 2, NYL, NZL), bf16),
-            pltpu.VMEM((BLK * NYL, NZL), f32),
+            pltpu.VMEM((BLK * PITCH, NZL), f32),
             pltpu.VMEM((NYL // 4 * BLK, 4 * NZL), bf16),
             pltpu.VMEM((BX * BZ + 1, BLK, BLK * BLK), bf16),
             pltpu.VMEM((slots, BLK, BLK * BLK), bf16),

time: 93 us -> 92 us (0.989)
  Pallas kernels: 43.2 us -> 42.2 us
    pallas_call x1, Pallas kernels: 25.6 us -> 24.5 us  [run_ions(): pl.pallas_call(ion_kernel, in_specs=[pl.BlockSpec(memory_space=pltpu.SMEM...]
where the time goes in v5:
time: 92 us; the launch traced here: 90.8 us
  Pallas kernels  42.2 us (46%)
  waiting for transfers between devices  38.5 us (42%)
  starting transfers between devices  9.47 us (10%)
    all_to_all x1, waiting for transfers between devices, per_device(): lax.all_to_all(outgoing, 'tile', split_axis=0, concat_axis=0, tiled=True)  38.5 us
    pallas_call x1, Pallas kernels, run_ions(): pl.pallas_call(ion_kernel, in_specs=[pl.BlockSpec(memory_space=pltpu.SMEM...  24.5 us
    pallas_call x1, Pallas kernels, run_flow(): pl.pallas_call(flow_kernel, grid=(BX,), in_specs=[any_spec(), any_spec(),...  13.8 us
    all_to_all x1, starting transfers between devices, per_device(): lax.all_to_all(outgoing, 'tile', split_axis=0, concat_axis=0, tiled=True)  9.47 us
    pallas_call x1, Pallas kernels, put_owned(): pl.pallas_call(owned_kernel, in_specs=[any_spec()], out_specs=any_spec(),...  3.85 us
  transfers between devices with their start and end apart: 1, of which 1 were waited for; matrix products, arithmetic and copies ran while one was open for 0% of the time, Pallas kernels for 15%

profile of v5, /device:TPU:1, one launch (start us, length us, event | category | flops | bytes accessed | tf_op | source)
XLA Modules:
  0.0 90.8 jit_solution(4642217921593949227)
XLA Ops:
  0.6 24.5 %ions.1 = (bf16[2,192,32,128]{3,2,1,0:T(8,128)(2,1)}, bf16[64,32,1024]{2,1,0:T(8,128)(2,1)}, bf16[2,7,192,128]{3,2,1,0:T(8,128)(2,1)}, bf16[2,4,32,128]{3,2,1,0:T(8,128)(2,1)}) custom-call(s32[24]{0:T(128)} %bitcast.4, bf16[2,192,32,128]{3,2,1,0:T(8,128)(2,1)} %conc_ref.1, bf16[192,32,128]{2,1,0:T(8,128)(2,1)} %pot_ref.3, bf16[192,32,128]{2,1,0:T(8,128)(2,1)} %diff_ref.1, ...), custom_call_target="tpu_custom_call" | custom-call | flops 200000000 | bytes 17000000 | tf_op jit(solution)/shard_map/ions/pallas_call | solution.py:445
  25.2 9.5 %all-to-all-start = ((bf16[32,2,32,1024]{3,2,1,0:T(8,128)(2,1)}), bf16[32,2,32,1024]{3,2,1,0:T(8,128)(2,1)}, u32[]{:S(2)}, u32[]{:S(2)}) async-start(bf16[32,2,32,1024]{3,2,1,0:T(8,128)(2,1)} %bitcast.3), calls=%async_computation | async-start | bytes 8388608 | tf_op jit(solution)/shard_map/all_to_all | solution.py:568
  34.6 13.8 %flow.1 = (bf16[3,192,32,128]{3,2,1,0:T(8,128)(2,1)}, bf16[2,192,32,128]{3,2,1,0:T(8,128)(2,1)}) custom-call(bf16[3,192,32,128]{3,2,1,0:T(8,128)(2,1)} %vel_ref.3, bf16[192,32,128]{2,1,0:T(8,128)(2,1)} %pot_ref.3, s32[192,32,128]{2,1,0:T(8,128)} %spacer_ref.3, bf16[2,192,32,128]{3,2,1,0:T(8,128)(2,1)} %get-tuple-element.9.conc_ref, ...), custom_call_target="tpu_custom_call" | custom-call | flops 200000000 | bytes 17000000 | tf_op jit(solution)/shard_map/flow/pallas_call | solution.py:528
  48.4 38.5 %all-to-all-done = bf16[32,2,32,1024]{3,2,1,0:T(8,128)(2,1)} async-done(((bf16[32,2,32,1024]{3,2,1,0:T(8,128)(2,1)}), bf16[32,2,32,1024]{3,2,1,0:T(8,128)(2,1)}, u32[]{:S(2)}, u32[]{:S(2)}) %all-to-all-start) | async-done | bytes 4194336 | tf_op jit(solution)/shard_map/all_to_all | solution.py:568
  86.9 3.8 %owned.1 = bf16[64,32,1024]{2,1,0:T(8,128)(2,1)} custom-call(bf16[64,32,1024]{2,1,0:T(8,128)(2,1)} %bitcast.2.part_ref), custom_call_target="tpu_custom_call" | custom-call | bytes 8400000 | tf_op jit(solution)/shard_map/owned/pallas_call | solution.py:509
Async XLA Ops:
  25.2 61.8 %all-to-all-start = ((bf16[32,2,32,1024]{3,2,1,0:T(8,128)(2,1)}), bf16[32,2,32,1024]{3,2,1,0:T(8,128)(2,1)}, u32[]{:S(2)}, u32[]{:S(2)}) async-start(bf16[32,2,32,1024]{3,2,1,0:T(8,128)(2,1)} %bitcast.3), calls=%async_computation | async-start | bytes 8388608 | tf_op jit(solution)/shard_map/all_to_all | solution.py:568
